TPU v7x, 256 devices: a whole 4x4x8 slice. The times are simulated.
256 devices in a mesh: bins: 64 (over z, y, core), slab: 4 (over x).
Axes of the slice: x: 4, y: 4, z: 8, core: 2. Of those that a mesh axis runs over, the one named last changes fastest.
Arguments:
- images: bfloat16 [1024, 128, 128], P('bins'), may hold values from -6 to 6
- projections: bfloat16 [512, 128, 128], P('bins'), may hold values from -6 to 6
- regions: int32 [1024, 2], P('bins'), may hold values from 0 to 63, all different within a row; in each aligned block of 16 rows (0 to 15, 16 to 31, ...) at most 2 rows name the same one
- offsets: int32 [2, 1024], P(None, 'bins'), may hold values from -12 to 12
- defocus: float32 [1024], P('bins'), may hold values from 0.5 to 3
- counts: int32 [512], P('bins'), may hold values from 0 to 399
- tilt_angle: float32 [512], P('bins'), may hold values from -3.140625 to 3.140625
Outputs:
- volume: float32 [128, 128, 128], P('bins', 'slab')
Inputs may be any that keep to these rules, and one draw needn't show every extreme that they name: The 2 regions of a particle differ. At most 2 of the 16 particles of one index of bins name the same region, and on some index exactly 2 do.
All inputs are finite; a program needn't handle non-finite values.
Results may differ from a plain program's by a relative error of at most 0.0046.
Values may be sent and summed in bfloat16 or wider, within the bound.
A program may use at most 64 MiB of HBM per device.

v0:
```python
import functools

import jax
import jax.numpy as jnp
import ml_dtypes
import numpy as np
from jax import lax
from jax.experimental import pallas as pl
from jax.experimental.pallas import tpu as pltpu
from jax.sharding import PartitionSpec as P

AMP_COS = 0.1
AMP_SIN = 0.99498743710662
CHI_SCALE = 100.0
ENVELOPE = 8.0
BOX = 128
PART = 16
BINS = 8
PLANE_GROUP = 8
MESH = pl.DeviceIdType.MESH
F32 = jnp.float32
BF16 = jnp.bfloat16


def tables(rows):
    i = np.arange(BOX)
    angle = 2.0 * np.pi / BOX * (i[:, None] * i[None, :] % BOX)
    cas = np.cos(angle) + np.sin(angle)
    high = cas.astype(ml_dtypes.bfloat16)
    low = (cas - high.astype(np.float64)).astype(ml_dtypes.bfloat16)
    right = np.concatenate([high, low], axis=1)
    left = np.concatenate([high, high, low], axis=1)
    last = np.concatenate([high, high, low], axis=0)
    wrapped = cas[np.arange(BOX + rows) % BOX].astype(np.float32)
    return right, left, last, wrapped


def split(value):
    high = value.astype(BF16)
    return high, (value - high.astype(F32)).astype(BF16)


def dot(a, b):
    return jnp.dot(a, b, preferred_element_type=F32)


def dot_nt(a, b):
    return lax.dot_general(a, b, (((1,), (1,)), ((), ())), preferred_element_type=F32)


def kernel(
    nz, nq, ns,
    offs, imgs, proj, meta, h_right, h_left, h_last, h_rows,
    out,
    gains, spec, staged, frames, refs, meta_p, meta_z, partial, stats, share, parts, total, aver, weights,
    give_e, give_o, take_e, take_o,
    s_mp, r_mp, s_pr, r_pr, s_mz, r_mz, s_rt, r_rt, s_lf, r_lf, s_x, r_x, s_st, r_st,
    s_rs, r_rs, s_ag, r_ag, s_e, r_e, s_o, r_o,
):
    rows = BOX // ns
    pairs = rows // 2
    half = rows // 2
    depth = 2 * nz * nq
    me = lax.axis_index("bins")
    slab = lax.axis_index("slab")
    z = me // nq
    q = lax.rem(me, nq)
    flip_q = nq - 1 - q
    centre = (BOX - 1) / 2.0

    def at_q(k):
        other = lax.rem(q + k, nq)
        return other, (z * nq + other, slab)

    def at_z(k):
        other = lax.rem(z + k, nz)
        return other, (other * nq + q, slab)

    barrier = pltpu.get_barrier_semaphore()
    partners = [at_q(k)[1] for k in range(1, nq)] + [at_z(k)[1] for k in range(1, nz)]
    partners += [(lax.rem(z + k, nz) * nq + flip_q, slab) for k in range(1, nz)]
    partners += [(me, lax.rem(slab + k, ns)) for k in range(1, ns)]
    for device in partners:
        pl.semaphore_signal(barrier, inc=1, device_id=device, device_id_type=MESH)

    lane = lax.broadcasted_iota(jnp.int32, (8, BOX), 1)
    meta_p[q, 0:8, :] = jnp.log(1.0 + meta[24:32, :])
    meta_p[q, 8:16, :] = jnp.cos(meta[16:24, :])
    meta_p[q, 16:24, :] = jnp.sin(meta[16:24, :])
    meta_z[z] = jnp.where(lane // PART == z, meta[32:40, :], 0.0)

    first_row = pl.multiple_of(slab * rows, rows)
    for g in range(BINS):
        staged[g * rows:(g + 1) * rows, :] = proj[g, pl.ds(first_row, rows), :].astype(F32)
    for r in range(pairs):
        even = staged[pl.ds(2 * r, BINS, stride=rows), :]
        odd = staged[pl.ds(2 * r + 1, BINS, stride=rows), :]
        refs[q, r] = jnp.concatenate([even, odd], axis=0).astype(BF16)

    index = lax.broadcasted_iota(jnp.int32, (PART, BOX), 1)
    freq = jnp.where(index < BOX // 2, index, index - BOX).astype(F32) / BOX
    square = freq * freq
    phase = CHI_SCALE * meta[0:PART, :] * square
    fade = jnp.exp(-ENVELOPE * square)
    sine, cosine = jnp.sin(phase), jnp.cos(phase)
    scale = -1.0 / (BOX * BOX)
    gains[0] = scale * fade * (AMP_SIN * sine + AMP_COS * cosine)
    gains[1] = scale * fade * (AMP_SIN * cosine - AMP_COS * sine)
    gains[2] = fade * cosine
    gains[3] = fade * sine

    def filter_one(p):
        t = dot(imgs[p], h_right[...])
        th, tl = split(t[:, :BOX] + t[:, BOX:])
        s = dot(h_left[...], jnp.concatenate([th, tl, th], axis=0))
        start = lax.rem(slab * rows - offs[0, p] + 2 * BOX, BOX)
        a = h_rows[pl.ds(start, rows), :]
        lh, ll = split(jnp.concatenate([a * gains[0, pl.ds(p, 1), :], a * gains[1, pl.ds(p, 1), :]], axis=1))
        rh, rl = split(jnp.concatenate([s * gains[2, pl.ds(p, 1), :], s * gains[3, pl.ds(p, 1), :]], axis=0))
        spec[pl.ds(pl.multiple_of(p * rows, rows), rows), :] = dot(lh, rh) + dot(lh, rl) + dot(ll, rh)

    def filter_some(step, carry):
        for k in range(4):
            filter_one(step * 4 + k)
        return carry

    lax.fori_loop(0, PART // 4, filter_some, 0)
    qh, ql = split(spec[...])
    plain = dot(jnp.concatenate([qh, ql, qh], axis=1), h_last[...])
    for p in range(PART):
        shift = lax.rem(offs[1, p] + BOX, BOX)
        staged[p * rows:(p + 1) * rows, :] = pltpu.roll(plain[p * rows:(p + 1) * rows, :], shift, 1)
    for r in range(rows):
        frames[z, r] = staged[pl.ds(r, PART, stride=rows), :].astype(BF16)

    pl.semaphore_wait(barrier, len(partners))

    def to_q(buf, send, recv, k):
        device = at_q(k)[1]
        return pltpu.make_async_remote_copy(buf.at[q], buf.at[q], send.at[k], recv.at[k], device_id=device, device_id_type=MESH)

    def to_z(buf, send, recv, k):
        device = at_z(k)[1]
        return pltpu.make_async_remote_copy(buf.at[z], buf.at[z], send.at[k], recv.at[k], device_id=device, device_id_type=MESH)

    def ring(step, sign, send, recv):
        source = lax.rem(z + (nz - sign * (step // 2)), nz)
        piece = step % 2 if sign > 0 else 1 - step % 2
        ref = frames.at[source, pl.ds(piece * half, half)]
        device = (lax.rem(z + nz + sign, nz) * nq + q, slab)
        return pltpu.make_async_remote_copy(ref, ref, send.at[step], recv.at[step], device_id=device, device_id_type=MESH)

    def right(step):
        return ring(step, 1, s_rt, r_rt)

    def left(step):
        return ring(step, -1, s_lf, r_lf)

    steps = nz - 1
    for step in range(min(2, steps)):
        right(step).start()
        left(step).start()
    for k in range(1, nq):
        to_q(meta_p, s_mp, r_mp, k).start()
    for k in range(1, nz):
        to_z(meta_z, s_mz, r_mz, k).start()
    for k in range(1, nq):
        to_q(refs, s_pr, r_pr, k).start()
    for k in range(1, nq):
        to_q(meta_p, s_mp, r_mp, k).wait()

    column = lax.broadcasted_iota(jnp.int32, (1, BOX), 1).astype(F32) - centre
    height = lax.broadcasted_iota(jnp.int32, (BOX, BOX), 0).astype(F32)

    def weigh(j):
        def one(g, carry):
            cosr = meta_p[j, pl.ds(8 + g, 1), :]
            sinr = meta_p[j, pl.ds(16 + g, 1), :]
            base = pl.multiple_of((j * BINS + g) * BOX, BOX)
            for k in range(nz):
                plane = 2 * (lax.rem(z + k, nz) * nq + q)
                away = plane.astype(F32) - (depth - 1) / 2.0
                landing = column * cosr + away * sinr + centre
                w = jnp.maximum(0.0, 1.0 - jnp.abs(landing - height))
                weights[pl.ds(base, BOX), k * BOX:(k + 1) * BOX] = w.astype(BF16)
            return carry

        lax.fori_loop(0, BINS, one, 0)

    for step in range(steps):
        right(step).wait_recv()
        if step + 2 < steps:
            right(step + 2).start()
        left(step).wait_recv()
        if step + 2 < steps:
            left(step + 2).start()
        if step < nq:
            weigh(step)
    for j in range(steps, nq):
        weigh(j)

    for k in range(1, nq):
        to_q(refs, s_pr, r_pr, k).wait()
    for k in range(1, nz):
        to_z(meta_z, s_mz, r_mz, k).wait()
    for step in range(steps):
        right(step).wait_send()
        left(step).wait_send()

    lanes = nz * PART

    def frame(r):
        return frames[:, r].reshape(lanes, BOX)

    def score(r, carry):
        even, odd = carry
        a = refs[:, r].reshape(nq * 2 * BINS, BOX)
        return even + dot_nt(a, frame(2 * r)), odd + dot_nt(a, frame(2 * r + 1))

    zero = jnp.zeros((nq * 2 * BINS, lanes), F32)
    even, odd = lax.fori_loop(0, pairs, score, (zero, zero), unroll=4)
    even = even.reshape(nq, 2, BINS, lanes)[:, 0]
    odd = odd.reshape(nq, 2, BINS, lanes)[:, 1]
    partial[slab] = (even + odd).reshape(nq * BINS, lanes)

    def to_x(k):
        device = (me, lax.rem(slab + k, ns))
        return pltpu.make_async_remote_copy(
            partial.at[slab], partial.at[slab], s_x.at[k], r_x.at[k], device_id=device, device_id_type=MESH
        )

    for k in range(1, ns):
        to_x(k).start()
    for k in range(1, ns):
        to_x(k).wait()
    scores = partial[0]
    for k in range(1, ns):
        scores = scores + partial[k]
    prior = meta_p[:, 0:8, :][:, :, :lanes].reshape(nq * BINS, lanes)
    logits = scores / BOX + prior
    named = meta_z[0]
    for k in range(1, nz):
        named = named + meta_z[k]
    owner = (lax.broadcasted_iota(jnp.int32, (nq * BINS, lanes), 0) // BINS + z * nq).astype(F32)
    wanted = (owner == named[0:1, :lanes]) | (owner == named[1:2, :lanes])
    low = jnp.float32(-3.0e38)
    top = jnp.max(jnp.where(wanted, logits, low), axis=0, keepdims=True)
    summed = jnp.sum(jnp.where(wanted, jnp.exp(jnp.where(wanted, logits - top, 0.0)), 0.0), axis=0, keepdims=True)
    stats[z, 0:1, :lanes] = top
    stats[z, 1:2, :lanes] = summed
    for k in range(1, nz):
        to_z(stats, s_st, r_st, k).start()
    for k in range(1, nz):
        to_z(stats, s_st, r_st, k).wait()
    tops = stats[:, 0, :lanes]
    sums = stats[:, 1, :lanes]
    best = jnp.max(tops, axis=0, keepdims=True)
    norm = best + jnp.log(jnp.sum(sums * jnp.exp(tops - best), axis=0, keepdims=True))
    posterior = jnp.where(wanted, jnp.exp(jnp.where(wanted, logits - norm, 0.0)), 0.0).astype(BF16)

    def average(r, carry):
        a = dot(posterior, frame(2 * r)).reshape(nq, BINS, BOX)
        b = dot(posterior, frame(2 * r + 1)).reshape(nq, BINS, BOX)
        share[:, r] = jnp.concatenate([a, b], axis=1).astype(BF16)
        return carry

    lax.fori_loop(0, pairs, average, 0, unroll=4)

    def to_owner(k):
        other, device = at_q(k)
        return pltpu.make_async_remote_copy(
            share.at[other], parts.at[k], s_rs.at[k], r_rs.at[k], device_id=device, device_id_type=MESH
        )

    for k in range(1, nq):
        to_owner(k).start()
    for k in range(1, nq):
        to_owner(k).wait()

    def add_up(r, carry):
        value = share[q, r].astype(F32)
        for k in range(1, nq):
            value = value + parts[k, r].astype(F32)
        total[pl.ds(pl.multiple_of(r * 2 * BINS, 2 * BINS), 2 * BINS), :] = value
        return carry

    lax.fori_loop(0, pairs, add_up, 0, unroll=4)
    mine = pl.multiple_of(q * BINS * BOX, BINS * BOX)
    for g in range(BINS):
        block = total[pl.ds(g, rows, stride=BINS), :].astype(BF16)
        aver[0:rows, pl.ds(pl.multiple_of(mine + g * BOX, BOX), BOX)] = block

    def to_group(k):
        ref = aver.at[pl.ds(0, rows), pl.ds(mine, BINS * BOX)]
        device = at_q(k)[1]
        return pltpu.make_async_remote_copy(ref, ref, s_ag.at[k], r_ag.at[k], device_id=device, device_id_type=MESH)

    for k in range(1, nq):
        to_group(k).start()

    mirror = (
        lax.broadcasted_iota(jnp.int32, (BOX, BOX), 0) + lax.broadcasted_iota(jnp.int32, (BOX, BOX), 1) == BOX - 1
    ).astype(F32).astype(BF16)

    def reverse(k):
        base = pl.multiple_of(lax.rem(q - k + nq, nq) * BINS * BOX, BINS * BOX)
        for g in range(BINS):
            at = pl.ds(pl.multiple_of(base + g * BOX, BOX), BOX)
            aver[rows:2 * rows, at] = dot(aver[0:rows, at], mirror).astype(BF16)

    reverse(0)
    for k in range(1, nq):
        to_group(k).wait()
        reverse(k)

    def even_copy(k):
        return pltpu.make_async_remote_copy(
            give_e.at[k], take_e.at[k], s_e.at[k], r_e.at[k], device_id=at_z(k)[1], device_id_type=MESH
        )

    def odd_copy(k):
        device = ((nz - 1 - lax.rem(z + k, nz)) * nq + flip_q, slab)
        return pltpu.make_async_remote_copy(
            give_o.at[k], take_o.at[k], s_o.at[k], r_o.at[k], device_id=device, device_id_type=MESH
        )

    order = sorted(range(nz // 2), key=lambda pair: -min(2 * pair, nz - 2 * pair))
    for pair in order:
        block = dot(aver[...], weights[:, 2 * pair * BOX:(2 * pair + 2) * BOX])
        for k in (2 * pair, 2 * pair + 1):
            at = (k - 2 * pair) * BOX
            give_e[k] = block[:rows, at:at + BOX].astype(BF16)
            give_o[k] = block[rows:, at:at + BOX].astype(BF16)
            odd_copy(k).start()
            if k:
                even_copy(k).start()

    for k in range(nz):
        odd_copy(k).wait()
        if k:
            even_copy(k).wait()
    value = give_e[0].astype(F32)
    for k in range(1, nz):
        value = value + take_e[k].astype(F32)
    out[0] = value
    value = take_o[0].astype(F32)
    for k in range(1, nz):
        value = value + take_o[k].astype(F32)
    high, rest = split(value)
    middle = (value - high.astype(F32)).astype(BF16)
    lowest = (value - high.astype(F32) - middle.astype(F32)).astype(BF16)
    out[1] = dot(jnp.concatenate([high, middle, lowest], axis=1), jnp.concatenate([mirror] * 3, axis=0))


def body(nz, nq, ns, images, projections, regions, offsets, defocus, counts, tilt_angle):
    rows = BOX // ns
    pairs = rows // 2
    wide = lambda vector: jnp.broadcast_to(vector.astype(F32)[:, None], (vector.shape[0], BOX))
    named = jnp.tile(regions.astype(F32).T, (1, BOX // PART))
    meta = jnp.concatenate(
        [wide(defocus), wide(tilt_angle), wide(counts), jnp.pad(named, ((0, 6), (0, 0)))], axis=0
    )
    vmem = pl.BlockSpec(memory_space=pltpu.VMEM)
    dma = pltpu.SemaphoreType.DMA
    scratch = [
        pltpu.VMEM((4, PART, BOX), F32),
        pltpu.VMEM((PART * rows, BOX), F32),
        pltpu.VMEM((PART * rows, BOX), F32),
        pltpu.VMEM((nz, rows, PART, BOX), BF16),
        pltpu.VMEM((nq, pairs, 2 * BINS, BOX), BF16),
        pltpu.VMEM((nq, 24, BOX), F32),
        pltpu.VMEM((nz, 8, BOX), F32),
        pltpu.VMEM((ns, nq * BINS, nz * PART), F32),
        pltpu.VMEM((nz, 8, BOX), F32),
        pltpu.VMEM((nq, pairs, 2 * BINS, BOX), BF16),
        pltpu.VMEM((nq, pairs, 2 * BINS, BOX), BF16),
        pltpu.VMEM((rows * BINS, BOX), F32),
        pltpu.VMEM((2 * rows, nq * BINS * BOX), BF16),
        pltpu.VMEM((nq * BINS * BOX, nz * BOX), BF16),
        pltpu.VMEM((nz, rows, BOX), BF16),
        pltpu.VMEM((nz, rows, BOX), BF16),
        pltpu.VMEM((nz, rows, BOX), BF16),
        pltpu.VMEM((nz, rows, BOX), BF16),
    ]
    for count in (nq, nq, nz, nz, nz, ns, nz, nq, nq, nz, nz):
        scratch += [dma((count,)), dma((count,))]
    return pl.pallas_call(
        functools.partial(kernel, nz, nq, ns),
        out_shape=jax.ShapeDtypeStruct((2, rows, BOX), F32),
        in_specs=[pl.BlockSpec(memory_space=pltpu.SMEM)] + [vmem] * 7,
        out_specs=vmem,
        scratch_shapes=scratch,
        compiler_params=pltpu.CompilerParams(
            collective_id=0, has_side_effects=True, vmem_limit_bytes=48 * 1024 * 1024
        ),
    )(offsets, images, projections, meta, *(jnp.asarray(table) for table in tables(rows)))


def solution(mesh):
    nq = PLANE_GROUP
    nz = mesh.shape["bins"] // nq
    ns = mesh.shape["slab"]
    in_specs = (
        P("bins", None, None),
        P("bins", None, None),
        P("bins", None),
        P(None, "bins"),
        P("bins"),
        P("bins"),
        P("bins"),
    )
    return jax.shard_map(
        functools.partial(body, nz, nq, ns),
        mesh=mesh,
        in_specs=in_specs,
        out_specs=P("bins", "slab", None),
        check_vma=False,
    )
```

profile of v0, /device:TPU:1, one launch (start us, length us, event | category | flops | bytes accessed | tf_op | source)
XLA Modules:
  0.0 79.2 jit_solution(12327565384587879881)
XLA Ops:
  0.0 0.0 copy-start.8
  0.0 0.0 copy-start.9
  0.0 0.7 convert_element_type.8
  0.7 0.0 copy-done.8
  0.7 0.0 copy-done.9
  0.7 0.0 copy-start.7
  0.7 0.1 maximum_maximum_fusion
  0.8 0.6 copy-done.7
  1.4 0.1 tile.10
  1.5 0.0 copy-start.6
  1.5 0.1 select_maximum_fusion.meta
  1.5 0.6 copy-done.6
  2.1 0.0 copy-start
  2.2 1.0 %copy-done = bf16[16,128,128]{2,1,0:T(8,128)(2,1)S(1)} copy-done((bf16[16,128,128]{2,1,0:T(8,128)(2,1)S(1)}, bf16[16,128,128]{2,1,0:T(8,128)(2,1)}, u32[]{:S(2)}) %copy-start) | copy-done | bytes 524312
  3.2 0.0 copy-start.1
  3.2 0.9 %copy-done.1 = bf16[8,128,128]{2,1,0:T(8,128)(2,1)S(1)} copy-done((bf16[8,128,128]{2,1,0:T(8,128)(2,1)S(1)}, bf16[8,128,128]{2,1,0:T(8,128)(2,1)}, u32[]{:S(2)}) %copy-start.1) | copy-done | bytes 262168
  4.1 0.0 copy-start.2
  4.1 0.9 %copy-done.2 = bf16[384,128]{1,0:T(8,128)(2,1)S(1)} copy-done((bf16[384,128]{1,0:T(8,128)(2,1)S(1)}, bf16[384,128]{1,0:T(8,128)(2,1)}, u32[]{:S(2)}) %copy-start.2) | copy-done | bytes 98328
  5.0 0.0 copy-start.3
  5.0 0.9 %copy-done.3 = bf16[128,384]{1,0:T(8,128)(2,1)S(1)} copy-done((bf16[128,384]{1,0:T(8,128)(2,1)S(1)}, bf16[128,384]{1,0:T(8,128)(2,1)}, u32[]{:S(2)}) %copy-start.3) | copy-done | bytes 98328
  5.9 0.0 copy-start.4
  5.9 0.9 %copy-done.4 = f32[160,128]{1,0:T(8,128)S(1)} copy-done((f32[160,128]{1,0:T(8,128)S(1)}, f32[160,128]{1,0:T(8,128)}, u32[]{:S(2)}) %copy-start.4) | copy-done | bytes 81944
  6.8 0.0 copy-start.5
  6.8 0.8 %copy-done.5 = bf16[128,256]{1,0:T(8,128)(2,1)S(1)} copy-done((bf16[128,256]{1,0:T(8,128)(2,1)S(1)}, bf16[128,256]{1,0:T(8,128)(2,1)}, u32[]{:S(2)}) %copy-start.5) | copy-done | bytes 65560
  7.7 70.9 %shard_map.109 = f32[2,32,128]{2,1,0:T(8,128)S(1)} custom-call(s32[2,16]{1,0:T(2,128)S(1)} %copy-done.6, bf16[16,128,128]{2,1,0:T(8,128)(2,1)S(1)} %copy-done, bf16[8,128,128]{2,1,0:T(8,128)(2,1)S(1)} %copy-done.1, f32[40,128]{1,0:T(8,128)S(1)} %select_maximum_fusion.meta, bf16[128,256]{1,0:T(8,128)(2,1)S(1)} %copy-done.5, bf16[128,384]{1,0:T(8,128)(2,1)S(1)} %copy-done.3, ...), custom_call_target="tpu_custom_call" | custom-call | tf_op jit(solution)/shard_map/pallas_call | solution.py:387
  78.6 0.6 copy.13
  (2 shorter events, 0.0 us)
Async XLA Ops:
  0.0 0.7 copy-start.8
  0.0 0.7 copy-start.9
  0.7 0.7 copy-start.7
  1.5 0.7 copy-start.6
  2.1 1.0 %copy-start = (bf16[16,128,128]{2,1,0:T(8,128)(2,1)S(1)}, bf16[16,128,128]{2,1,0:T(8,128)(2,1)}, u32[]{:S(2)}) copy-start(bf16[16,128,128]{2,1,0:T(8,128)(2,1)} %imgs.1) | copy-start | bytes 1572868
  3.2 0.9 %copy-start.1 = (bf16[8,128,128]{2,1,0:T(8,128)(2,1)S(1)}, bf16[8,128,128]{2,1,0:T(8,128)(2,1)}, u32[]{:S(2)}) copy-start(bf16[8,128,128]{2,1,0:T(8,128)(2,1)} %proj.1) | copy-start | bytes 786436
  4.1 0.9 %copy-start.2 = (bf16[384,128]{1,0:T(8,128)(2,1)S(1)}, bf16[384,128]{1,0:T(8,128)(2,1)}, u32[]{:S(2)}) copy-start(bf16[384,128]{1,0:T(8,128)(2,1)} %constant.13.clone.h_last) | copy-start | bytes 294916
  5.0 0.9 %copy-start.3 = (bf16[128,384]{1,0:T(8,128)(2,1)S(1)}, bf16[128,384]{1,0:T(8,128)(2,1)}, u32[]{:S(2)}) copy-start(bf16[128,384]{1,0:T(8,128)(2,1)} %constant.12.clone.h_left) | copy-start | bytes 294916
  5.9 0.9 %copy-start.4 = (f32[160,128]{1,0:T(8,128)S(1)}, f32[160,128]{1,0:T(8,128)}, u32[]{:S(2)}) copy-start(f32[160,128]{1,0:T(8,128)} %constant.14.clone.h_rows) | copy-start | bytes 245764
  6.8 0.8 %copy-start.5 = (bf16[128,256]{1,0:T(8,128)(2,1)S(1)}, bf16[128,256]{1,0:T(8,128)(2,1)}, u32[]{:S(2)}) copy-start(bf16[128,256]{1,0:T(8,128)(2,1)} %constant.11.clone.h_right) | copy-start | bytes 196612
where the time goes:
time: 79.6 us; the launch traced here: 79.2 us
  Pallas kernels  70.9 us (89%)
  local copies, waits for them, and re-layouts  7.42 us (9%)
  other arithmetic  0.84 us (1%)
    pallas_call x1, Pallas kernels, body(): pl.pallas_call(functools.partial(kernel, nz, nq, ns), out_shape=jax.Shape...  70.9 us
    unnamed x21, local copies, waits for them, and re-layouts  7.33 us

commit v1 on v0

v1 whole, which is shorter than its diff:
```python
import functools

import jax
import jax.numpy as jnp
import ml_dtypes
import numpy as np
from jax import lax
from jax.experimental import pallas as pl
from jax.experimental.pallas import tpu as pltpu
from jax.sharding import PartitionSpec as P

AMP_COS = 0.1
AMP_SIN = 0.99498743710662
CHI_SCALE = 100.0
ENVELOPE = 8.0
BOX = 128
PART = 16
BINS = 8
PLANE_GROUP = 8
PIECES = 4
MESH = pl.DeviceIdType.MESH
F32 = jnp.float32
BF16 = jnp.bfloat16


def tables(rows):
    i = np.arange(BOX)
    angle = 2.0 * np.pi / BOX * (i[:, None] * i[None, :] % BOX)
    cas = np.cos(angle) + np.sin(angle)
    high = cas.astype(ml_dtypes.bfloat16)
    low = (cas - high.astype(np.float64)).astype(ml_dtypes.bfloat16)
    right = np.concatenate([high, low], axis=1)
    left = np.concatenate([high, high, low], axis=1)
    last = np.concatenate([high, high, low], axis=0)
    wrapped = cas[np.arange(BOX + rows) % BOX].astype(np.float32)
    return right, left, last, wrapped


def split(value):
    high = value.astype(BF16)
    return high, (value - high.astype(F32)).astype(BF16)


def dot(a, b):
    return jnp.dot(a, b, preferred_element_type=F32)


def dot_nt(a, b):
    return lax.dot_general(a, b, (((1,), (1,)), ((), ())), preferred_element_type=F32)


def kernel(
    nz, nq, ns,
    regions, offs, defocus, counts, tilt, images_hbm, proj_hbm, right_hbm, left_hbm, last_hbm, rows_hbm,
    out,
    imgs, proj, h_right, h_left, h_last, h_rows,
    gains, spec, staged, frames, refs, meta_p, meta_z, partial, stats, share, from_core, send_y, from_y, total,
    aver, weights, planes, give_e, give_o, take_e, take_o,
    s_in, s_mp, r_mp, s_pr, r_pr, s_mz, r_mz, s_rt, r_rt, s_lf, r_lf, s_x, r_x, s_st, r_st,
    s_rc, r_rc, s_ry, r_ry, s_ac, r_ac, s_ay, r_ay, s_e, r_e, s_o, r_o,
):
    rows = BOX // ns
    pairs = rows // 2
    ny = nq // 2
    quarter = rows // PIECES
    depth = 2 * nz * nq
    me = lax.axis_index("bins")
    slab = lax.axis_index("slab")
    z = me // nq
    q = lax.rem(me, nq)
    flip_q = nq - 1 - q
    y = q // 2
    core = lax.rem(q, 2)
    other_core = (z * nq + 2 * y + 1 - core, slab)
    centre = (BOX - 1) / 2.0

    def at_q(k):
        other = lax.rem(q + k, nq)
        return other, (z * nq + other, slab)

    def at_z(k):
        other = lax.rem(z + k, nz)
        return other, (other * nq + q, slab)

    def at_y(k):
        other = lax.rem(y + k, ny)
        return other, (z * nq + 2 * other + core, slab)

    first_row = pl.multiple_of(slab * rows, rows)
    loads = [
        pltpu.make_async_copy(src, dst, s_in.at[i])
        for i, (src, dst) in enumerate(
            (
                (images_hbm, imgs),
                (right_hbm, h_right),
                (left_hbm, h_left),
                (rows_hbm, h_rows),
                (last_hbm, h_last),
                (proj_hbm.at[:, pl.ds(first_row, rows)], proj),
            )
        )
    ]
    for load in loads:
        load.start()

    barrier = pltpu.get_barrier_semaphore()
    partners = [at_q(k)[1] for k in range(1, nq)] + [at_z(k)[1] for k in range(1, nz)]
    partners += [(lax.rem(z + k, nz) * nq + flip_q, slab) for k in range(1, nz)]
    partners += [(me, lax.rem(slab + k, ns)) for k in range(1, ns)]
    for device in partners:
        pl.semaphore_signal(barrier, inc=1, device_id=device, device_id_type=MESH)

    lane = lax.broadcasted_iota(jnp.int32, (8, BOX), 1)
    line = lax.broadcasted_iota(jnp.int32, (8, BOX), 0)
    angle = jnp.zeros((8, BOX), F32)
    count = jnp.zeros((8, BOX), jnp.int32)
    for g in range(BINS):
        angle = jnp.where(line == g, tilt[g], angle)
        count = jnp.where(line == g, counts[g], count)
    meta_p[q, 0:8, :] = jnp.log(1.0 + count.astype(F32))
    meta_p[q, 8:16, :] = jnp.cos(angle)
    meta_p[q, 16:24, :] = jnp.sin(angle)
    named = jnp.zeros((8, BOX), jnp.int32)
    for p in range(PART):
        for t in range(2):
            named = jnp.where((lane == z * PART + p) & (line == t), regions[p, t], named)
    meta_z[z] = named

    index = lax.broadcasted_iota(jnp.int32, (PART, BOX), 1)
    which = lax.broadcasted_iota(jnp.int32, (PART, BOX), 0)
    blur = jnp.zeros((PART, BOX), F32)
    for p in range(PART):
        blur = jnp.where(which == p, defocus[p], blur)
    freq = jnp.where(index < BOX // 2, index, index - BOX).astype(F32) / BOX
    square = freq * freq
    phase = CHI_SCALE * blur * square
    fade = jnp.exp(-ENVELOPE * square)
    sine, cosine = jnp.sin(phase), jnp.cos(phase)
    scale = -1.0 / (BOX * BOX)
    gains[0] = scale * fade * (AMP_SIN * sine + AMP_COS * cosine)
    gains[1] = scale * fade * (AMP_SIN * cosine - AMP_COS * sine)
    gains[2] = fade * cosine
    gains[3] = fade * sine

    loads[5].wait()
    for g in range(BINS):
        staged[g * rows:(g + 1) * rows, :] = proj[g].astype(F32)
    for r in range(pairs):
        even = staged[pl.ds(2 * r, BINS, stride=rows), :]
        odd = staged[pl.ds(2 * r + 1, BINS, stride=rows), :]
        refs[q, r] = jnp.concatenate([even, odd], axis=0).astype(BF16)

    def filter_one(p):
        t = dot(imgs[p], h_right[...])
        th, tl = split(t[:, :BOX] + t[:, BOX:])
        s = dot(h_left[...], jnp.concatenate([th, tl, th], axis=0))
        start = lax.rem(slab * rows - offs[0, p] + 2 * BOX, BOX)
        a = h_rows[pl.ds(start, rows), :]
        lh, ll = split(jnp.concatenate([a * gains[0, pl.ds(p, 1), :], a * gains[1, pl.ds(p, 1), :]], axis=1))
        rh, rl = split(jnp.concatenate([s * gains[2, pl.ds(p, 1), :], s * gains[3, pl.ds(p, 1), :]], axis=0))
        spec[pl.ds(pl.multiple_of(p * rows, rows), rows), :] = dot(lh, rh) + dot(lh, rl) + dot(ll, rh)

    def filter_some(step, carry):
        for k in range(4):
            filter_one(step * 4 + k)
        return carry

    for load in loads[:4]:
        load.wait()
    lax.fori_loop(0, PART // 4, filter_some, 0)
    loads[4].wait()
    qh, ql = split(spec[...])
    plain = dot(jnp.concatenate([qh, ql, qh], axis=1), h_last[...])
    for p in range(PART):
        shift = lax.rem(offs[1, p] + BOX, BOX)
        staged[p * rows:(p + 1) * rows, :] = pltpu.roll(plain[p * rows:(p + 1) * rows, :], shift, 1)
    for r in range(rows):
        frames[z, r] = staged[pl.ds(r, PART, stride=rows), :].astype(BF16)

    pl.semaphore_wait(barrier, len(partners))

    def to_q(buf, send, recv, k):
        device = at_q(k)[1]
        return pltpu.make_async_remote_copy(buf.at[q], buf.at[q], send.at[k], recv.at[k], device_id=device, device_id_type=MESH)

    def to_z(buf, send, recv, k):
        device = at_z(k)[1]
        return pltpu.make_async_remote_copy(buf.at[z], buf.at[z], send.at[k], recv.at[k], device_id=device, device_id_type=MESH)

    def ring(step, sign, send, recv):
        source = lax.rem(z + (nz - sign * (step // PIECES)), nz)
        piece = step % PIECES if sign > 0 else PIECES - 1 - step % PIECES
        ref = frames.at[source, pl.ds(piece * quarter, quarter)]
        device = (lax.rem(z + nz + sign, nz) * nq + q, slab)
        return pltpu.make_async_remote_copy(ref, ref, send.at[step], recv.at[step], device_id=device, device_id_type=MESH)

    def right(step):
        return ring(step, 1, s_rt, r_rt)

    def left(step):
        return ring(step, -1, s_lf, r_lf)

    steps = PIECES * (nz - 1) // 2
    for step in range(PIECES):
        right(step).start()
        left(step).start()
    for k in range(1, nq):
        to_q(meta_p, s_mp, r_mp, k).start()
    for k in range(1, nz):
        to_z(meta_z, s_mz, r_mz, k).start()
    for k in range(1, nq):
        to_q(refs, s_pr, r_pr, k).start()
    for k in range(1, nq):
        to_q(meta_p, s_mp, r_mp, k).wait()

    column = lax.broadcasted_iota(jnp.int32, (1, BOX), 1).astype(F32) - centre
    height = lax.broadcasted_iota(jnp.int32, (BOX, BOX), 0).astype(F32)

    def weigh(unit):
        j = unit // 2

        def one(g, carry):
            cosr = meta_p[j, pl.ds(8 + g, 1), :]
            sinr = meta_p[j, pl.ds(16 + g, 1), :]
            base = pl.multiple_of((j * BINS + g) * BOX, BOX)
            for k in range(nz):
                plane = 2 * (lax.rem(z + k, nz) * nq + q)
                away = plane.astype(F32) - (depth - 1) / 2.0
                landing = column * cosr + away * sinr + centre
                w = jnp.maximum(0.0, 1.0 - jnp.abs(landing - height))
                weights[pl.ds(base, BOX), k * BOX:(k + 1) * BOX] = w.astype(BF16)
            return carry

        first = unit % 2 * (BINS // 2)
        lax.fori_loop(first, first + BINS // 2, one, 0)

    units = 2 * nq
    for step in range(steps):
        right(step).wait_recv()
        if step + PIECES < steps:
            right(step + PIECES).start()
        left(step).wait_recv()
        if step + PIECES < steps:
            left(step + PIECES).start()
        for unit in range(step * units // steps, (step + 1) * units // steps):
            weigh(unit)

    for k in range(1, nq):
        to_q(refs, s_pr, r_pr, k).wait()
    for k in range(1, nz):
        to_z(meta_z, s_mz, r_mz, k).wait()
    for step in range(steps):
        right(step).wait_send()
        left(step).wait_send()

    lanes = nz * PART

    def frame(r):
        return frames[:, r].reshape(lanes, BOX)

    def score(r, carry):
        even, odd = carry
        a = refs[:, r].reshape(nq * 2 * BINS, BOX)
        return even + dot_nt(a, frame(2 * r)), odd + dot_nt(a, frame(2 * r + 1))

    zero = jnp.zeros((nq * 2 * BINS, lanes), F32)
    even, odd = lax.fori_loop(0, pairs, score, (zero, zero), unroll=4)
    even = even.reshape(nq, 2, BINS, lanes)[:, 0]
    odd = odd.reshape(nq, 2, BINS, lanes)[:, 1]
    scores = even + odd

    named = meta_z[0]
    for k in range(1, nz):
        named = named + meta_z[k]
    prior = meta_p[:, 0:8, :lanes]
    held, priors = [], []
    for t in range(2):
        place = named[t:t + 1, :lanes] - z * nq
        chosen = jnp.zeros((BINS, lanes), F32)
        chance = jnp.zeros((BINS, lanes), F32)
        for j in range(nq):
            chosen = jnp.where(place == j, scores[j], chosen)
            chance = jnp.where(place == j, prior[j], chance)
        partial[slab, t * BINS:(t + 1) * BINS, :] = chosen
        priors.append(chance)
        held.append((place >= 0) & (place < nq))

    def to_x(k):
        device = (me, lax.rem(slab + k, ns))
        return pltpu.make_async_remote_copy(
            partial.at[slab], partial.at[slab], s_x.at[k], r_x.at[k], device_id=device, device_id_type=MESH
        )

    for k in range(1, ns):
        to_x(k).start()
    for k in range(1, ns):
        to_x(k).wait()
    scores = partial[0]
    for k in range(1, ns):
        scores = scores + partial[k]
    low = jnp.float32(-3.0e38)
    logits = [scores[t * BINS:(t + 1) * BINS] / BOX + priors[t] for t in range(2)]
    tops = [jnp.where(held[t], jnp.max(logits[t], axis=0, keepdims=True), low) for t in range(2)]
    top = jnp.maximum(tops[0], tops[1])
    summed = jnp.zeros((1, lanes), F32)
    for t in range(2):
        grown = jnp.exp(jnp.where(held[t], logits[t] - top, low))
        summed = summed + jnp.sum(grown, axis=0, keepdims=True)
    stats[z, 0:1, :lanes] = top
    stats[z, 1:2, :lanes] = summed
    for k in range(1, nz):
        to_z(stats, s_st, r_st, k).start()
    for k in range(1, nz):
        to_z(stats, s_st, r_st, k).wait()
    best = stats[0, 0:1, :lanes]
    for k in range(1, nz):
        best = jnp.maximum(best, stats[k, 0:1, :lanes])
    whole = jnp.zeros((1, lanes), F32)
    for k in range(nz):
        whole = whole + stats[k, 1:2, :lanes] * jnp.exp(stats[k, 0:1, :lanes] - best)
    norm = best + jnp.log(whole)
    chances = [jnp.exp(jnp.where(held[t], logits[t] - norm, low)) for t in range(2)]
    posterior = []
    for j in range(nq):
        value = jnp.zeros((BINS, lanes), F32)
        for t in range(2):
            place = named[t:t + 1, :lanes] - z * nq
            value = jnp.where(place == j, chances[t], value)
        posterior.append(value)
    posterior = jnp.concatenate(posterior, axis=0).astype(BF16)

    def average(r, carry):
        a = dot(posterior, frame(r)).reshape(ny, 2, BINS, BOX)
        share[0, :, r] = a[:, 0]
        share[1, :, r] = a[:, 1]
        return carry

    lax.fori_loop(0, rows, average, 0, unroll=8)

    def to_core(k):
        place = at_y(k)[0]
        return pltpu.make_async_remote_copy(
            share.at[1 - core, place], from_core.at[place], s_rc.at[k], r_rc.at[k],
            device_id=other_core, device_id_type=MESH,
        )

    def to_owner(k):
        return pltpu.make_async_remote_copy(
            send_y.at[k], from_y.at[k], s_ry.at[k], r_ry.at[k], device_id=at_y(k)[1], device_id_type=MESH
        )

    far_first = sorted(range(1, ny), key=lambda k: -min(k, ny - k))
    for k in far_first + [0]:
        to_core(k).start()
    for k in far_first:
        place = at_y(k)[0]
        to_core(k).wait_recv()

        def pack(r, carry):
            a = share[core, place, 2 * r] + from_core[place, 2 * r]
            b = share[core, place, 2 * r + 1] + from_core[place, 2 * r + 1]
            send_y[k, r] = jnp.concatenate([a, b], axis=0).astype(BF16)
            return carry

        lax.fori_loop(0, pairs, pack, 0, unroll=8)
        to_owner(k).start()
    to_core(0).wait_recv()
    for k in range(1, ny):
        to_owner(k).wait_recv()

    def add_up(r, carry):
        a = share[core, y, 2 * r] + from_core[y, 2 * r]
        b = share[core, y, 2 * r + 1] + from_core[y, 2 * r + 1]
        value = jnp.concatenate([a, b], axis=0)
        for k in range(1, ny):
            value = value + from_y[k, r].astype(F32)
        total[pl.ds(pl.multiple_of(r * 2 * BINS, 2 * BINS), 2 * BINS), :] = value
        return carry

    lax.fori_loop(0, pairs, add_up, 0, unroll=8)
    span = BINS * BOX
    mine = pl.multiple_of(q * span, span)
    for g in range(BINS):
        block = total[pl.ds(g, rows, stride=BINS), :].astype(BF16)
        aver[0:rows, pl.ds(pl.multiple_of(mine + g * BOX, BOX), BOX)] = block

    def block_of(place, which):
        return pl.multiple_of((2 * place + which) * span, span)

    def along_y(k):
        ref = aver.at[pl.ds(0, rows), pl.ds(mine, span)]
        return pltpu.make_async_remote_copy(ref, ref, s_ay.at[k], r_ay.at[k], device_id=at_y(k)[1], device_id_type=MESH)

    def across(k):
        ref = aver.at[pl.ds(0, rows), pl.ds(block_of(lax.rem(y - k + ny, ny), core), span)]
        return pltpu.make_async_remote_copy(ref, ref, s_ac.at[k], r_ac.at[k], device_id=other_core, device_id_type=MESH)

    for k in far_first:
        along_y(k).start()
    across(0).start()

    mirror = (
        lax.broadcasted_iota(jnp.int32, (BOX, BOX), 0) + lax.broadcasted_iota(jnp.int32, (BOX, BOX), 1) == BOX - 1
    ).astype(F32).astype(BF16)

    def reverse(base):
        tiles = [aver[0:rows, pl.ds(pl.multiple_of(base + g * BOX, BOX), BOX)] for g in range(BINS)]
        turned = dot(jnp.concatenate(tiles, axis=0), mirror).astype(BF16)
        for g in range(BINS):
            aver[rows:2 * rows, pl.ds(pl.multiple_of(base + g * BOX, BOX), BOX)] = turned[g * rows:(g + 1) * rows]

    def project(base, lanes_at):
        return dot(aver[:, pl.ds(base, span)], weights[pl.ds(base, span), lanes_at])

    def add_block(base, first):
        reverse(base)
        for pair in range(nz // 2):
            at = slice(2 * pair * BOX, (2 * pair + 2) * BOX)
            block = project(base, at)
            planes[:, at] = block if first else planes[:, at] + block

    near_first = far_first[::-1]
    add_block(block_of(y, core), True)
    across(0).wait_recv()
    add_block(block_of(y, 1 - core), False)
    for k in near_first:
        along_y(k).wait_recv()
        across(k).start()
        add_block(block_of(lax.rem(y - k + ny, ny), core), False)
        across(k).wait_recv()
        if k != near_first[-1]:
            add_block(block_of(lax.rem(y - k + ny, ny), 1 - core), False)
    final = block_of(lax.rem(y - near_first[-1] + ny, ny), 1 - core)
    reverse(final)

    def even_copy(k):
        return pltpu.make_async_remote_copy(
            give_e.at[k], take_e.at[k], s_e.at[k], r_e.at[k], device_id=at_z(k)[1], device_id_type=MESH
        )

    def odd_copy(k):
        device = ((nz - 1 - lax.rem(z + k, nz)) * nq + flip_q, slab)
        return pltpu.make_async_remote_copy(
            give_o.at[k], take_o.at[k], s_o.at[k], r_o.at[k], device_id=device, device_id_type=MESH
        )

    order = sorted(range(nz // 2), key=lambda pair: -min(2 * pair, nz - 2 * pair))
    for pair in order:
        at = slice(2 * pair * BOX, (2 * pair + 2) * BOX)
        block = planes[:, at] + project(final, at)
        for k in (2 * pair, 2 * pair + 1):
            at = (k - 2 * pair) * BOX
            give_e[k] = block[:rows, at:at + BOX].astype(BF16)
            give_o[k] = block[rows:, at:at + BOX].astype(BF16)
            odd_copy(k).start()
            if k:
                even_copy(k).start()

    for k in range(nz):
        odd_copy(k).wait()
        if k:
            even_copy(k).wait()
    for k in range(ny):
        to_core(k).wait_send()
        across(k).wait_send()
        if k:
            to_owner(k).wait_send()
            along_y(k).wait_send()
    value = give_e[0].astype(F32)
    for k in range(1, nz):
        value = value + take_e[k].astype(F32)
    out[0] = value
    value = take_o[0].astype(F32)
    for k in range(1, nz):
        value = value + take_o[k].astype(F32)
    high, rest = split(value)
    middle = (value - high.astype(F32)).astype(BF16)
    lowest = (value - high.astype(F32) - middle.astype(F32)).astype(BF16)
    out[1] = dot(jnp.concatenate([high, middle, lowest], axis=1), jnp.concatenate([mirror] * 3, axis=0))


def body(nz, nq, ns, images, projections, regions, offsets, defocus, counts, tilt_angle):
    rows = BOX // ns
    pairs = rows // 2
    ny = nq // 2
    vmem = pl.BlockSpec(memory_space=pltpu.VMEM)
    dma = pltpu.SemaphoreType.DMA
    scratch = [
        pltpu.VMEM((PART, BOX, BOX), BF16),
        pltpu.VMEM((BINS, rows, BOX), BF16),
        pltpu.VMEM((BOX, 2 * BOX), BF16),
        pltpu.VMEM((BOX, 3 * BOX), BF16),
        pltpu.VMEM((3 * BOX, BOX), BF16),
        pltpu.VMEM((BOX + rows, BOX), F32),
        pltpu.VMEM((4, PART, BOX), F32),
        pltpu.VMEM((PART * rows, BOX), F32),
        pltpu.VMEM((PART * rows, BOX), F32),
        pltpu.VMEM((nz, rows, PART, BOX), BF16),
        pltpu.VMEM((nq, pairs, 2 * BINS, BOX), BF16),
        pltpu.VMEM((nq, 24, BOX), F32),
        pltpu.VMEM((nz, 8, BOX), jnp.int32),
        pltpu.VMEM((ns, 2 * BINS, nz * PART), F32),
        pltpu.VMEM((nz, 8, BOX), F32),
        pltpu.VMEM((2, ny, rows, BINS, BOX), F32),
        pltpu.VMEM((ny, rows, BINS, BOX), F32),
        pltpu.VMEM((ny, pairs, 2 * BINS, BOX), BF16),
        pltpu.VMEM((ny, pairs, 2 * BINS, BOX), BF16),
        pltpu.VMEM((rows * BINS, BOX), F32),
        pltpu.VMEM((2 * rows, nq * BINS * BOX), BF16),
        pltpu.VMEM((nq * BINS * BOX, nz * BOX), BF16),
        pltpu.VMEM((2 * rows, nz * BOX), F32),
        pltpu.VMEM((nz, rows, BOX), BF16),
        pltpu.VMEM((nz, rows, BOX), BF16),
        pltpu.VMEM((nz, rows, BOX), BF16),
        pltpu.VMEM((nz, rows, BOX), BF16),
    ]
    scratch.append(dma((6,)))
    steps = PIECES * (nz - 1) // 2
    for count in (nq, nq, nz, steps, steps, ns, nz, ny, ny, ny, ny, nz, nz):
        scratch += [dma((count,)), dma((count,))]
    return pl.pallas_call(
        functools.partial(kernel, nz, nq, ns),
        out_shape=jax.ShapeDtypeStruct((2, rows, BOX), F32),
        in_specs=[pl.BlockSpec(memory_space=pltpu.SMEM)] * 5 + [pl.BlockSpec(memory_space=pl.ANY)] * 6,
        out_specs=vmem,
        scratch_shapes=scratch,
        compiler_params=pltpu.CompilerParams(
            collective_id=0, has_side_effects=True, vmem_limit_bytes=60 * 1024 * 1024
        ),
    )(regions, offsets, defocus, counts, tilt_angle, images, projections, *(jnp.asarray(table) for table in tables(rows)))


def solution(mesh):
    nq = PLANE_GROUP
    nz = mesh.shape["bins"] // nq
    ns = mesh.shape["slab"]
    in_specs = (
        P("bins", None, None),
        P("bins", None, None),
        P("bins", None),
        P(None, "bins"),
        P("bins"),
        P("bins"),
        P("bins"),
    )
    return jax.shard_map(
        functools.partial(body, nz, nq, ns),
        mesh=mesh,
        in_specs=in_specs,
        out_specs=P("bins", "slab", None),
        check_vma=False,
    )
```

time: 79.6 us -> 70.1 us (0.88)
  local copies, waits for them, and re-layouts: 7.42 us -> 2.73 us
  Pallas kernels: 70.9 us -> 67.1 us
  other arithmetic: 0.84 us -> 0 us
    unnamed x21 -> x2, local copies, waits for them, and re-layouts: 7.33 us -> 2.73 us
    pallas_call x1, Pallas kernels: 70.9 us -> 67.1 us  [body(): pl.pallas_call(functools.partial(kernel, nz, nq, ns), out_shape=jax.Shape...]
where the time goes in v1:
time: 70.1 us; the launch traced here: 69.9 us
  Pallas kernels  67.1 us (96%)
  local copies, waits for them, and re-layouts  2.73 us (4%)
    pallas_call x1, Pallas kernels, body(): pl.pallas_call(functools.partial(kernel, nz, nq, ns), out_shape=jax.Shape...  67.1 us
    unnamed x2, local copies, waits for them, and re-layouts  2.73 us

profile of v1, /device:TPU:1, one launch (start us, length us, event | category | flops | bytes accessed | tf_op | source)
XLA Modules:
  0.0 69.9 jit_solution(6345718252068134438)
XLA Ops:
  0.0 1.4 %copy.12.regions = s32[16,2]{1,0:T(8,128)} copy(s32[16,2]{0,1:T(2,128)} %param.13) | data formatting | bytes 256 | tf_op args[2]
  1.4 67.1 %shard_map.109 = f32[2,32,128]{2,1,0:T(8,128)} custom-call(s32[16,2]{1,0:T(8,128)} %copy.12.regions, s32[2,16]{1,0:T(2,128)} %offs.1, f32[16]{0:T(128)} %defocus.1, s32[8]{0:T(128)} %counts.1, f32[8]{0:T(128)} %tilt.1, bf16[16,128,128]{2,1,0:T(8,128)(2,1)} %images_hbm.1, bf16[8,128,128]{2,1,0:T(8,128)(2,1)} %proj_hbm.1, ...), custom_call_target="tpu_custom_call" | custom-call | tf_op jit(solution)/shard_map/pallas_call | solution.py:521
  68.5 1.4 %copy.14 = f32[2,32,128]{2,1,0:T(8,128)} copy(f32[2,32,128]{2,1,0:T(8,128)} %shard_map.109) | data formatting | bytes 65536

commit v2 on v1

--- a/solution.py
+++ b/solution.py
@@ -23,17 +23,12 @@
 BF16 = jnp.bfloat16
 
 
-def tables(rows):
+def cosine_table():
     i = np.arange(BOX)
-    angle = 2.0 * np.pi / BOX * (i[:, None] * i[None, :] % BOX)
-    cas = np.cos(angle) + np.sin(angle)
-    high = cas.astype(ml_dtypes.bfloat16)
-    low = (cas - high.astype(np.float64)).astype(ml_dtypes.bfloat16)
-    right = np.concatenate([high, low], axis=1)
-    left = np.concatenate([high, high, low], axis=1)
-    last = np.concatenate([high, high, low], axis=0)
-    wrapped = cas[np.arange(BOX + rows) % BOX].astype(np.float32)
-    return right, left, last, wrapped
+    cosine = np.cos(2.0 * np.pi / BOX * (i[:, None] * i[None, :] % BOX))
+    high = cosine.astype(ml_dtypes.bfloat16)
+    low = (cosine - high.astype(np.float64)).astype(ml_dtypes.bfloat16)
+    return np.concatenate([high, high, low], axis=0)
 
 
 def split(value):
@@ -51,10 +46,9 @@
 
 def kernel(
     nz, nq, ns,
-    regions, offs, defocus, counts, tilt, images_hbm, proj_hbm, right_hbm, left_hbm, last_hbm, rows_hbm,
+    regions, offs, defocus, counts, tilt, images_hbm, proj_hbm, table_hbm,
     out,
-    imgs, proj, h_right, h_left, h_last, h_rows,
-    gains, spec, staged, frames, refs, meta_p, meta_z, partial, stats, share, from_core, send_y, from_y, total,
+    imgs, proj, table, taps, staged, frames, refs, meta_p, meta_z, partial, stats, share, from_core, send_y, from_y, total,
     aver, weights, planes, give_e, give_o, take_e, take_o,
     s_in, s_mp, r_mp, s_pr, r_pr, s_mz, r_mz, s_rt, r_rt, s_lf, r_lf, s_x, r_x, s_st, r_st,
     s_rc, r_rc, s_ry, r_ry, s_ac, r_ac, s_ay, r_ay, s_e, r_e, s_o, r_o,
@@ -91,11 +85,8 @@
         pltpu.make_async_copy(src, dst, s_in.at[i])
         for i, (src, dst) in enumerate(
             (
+                (table_hbm, table),
                 (images_hbm, imgs),
-                (right_hbm, h_right),
-                (left_hbm, h_left),
-                (rows_hbm, h_rows),
-                (last_hbm, h_last),
                 (proj_hbm.at[:, pl.ds(first_row, rows)], proj),
             )
         )
@@ -123,7 +114,7 @@
     named = jnp.zeros((8, BOX), jnp.int32)
     for p in range(PART):
         for t in range(2):
-            named = jnp.where((lane == z * PART + p) & (line == t), regions[p, t], named)
+            named = jnp.where((lane == z * PART + p) & (line == t), regions[t, p], named)
     meta_z[z] = named
 
     index = lax.broadcasted_iota(jnp.int32, (PART, BOX), 1)
@@ -136,13 +127,22 @@
     phase = CHI_SCALE * blur * square
     fade = jnp.exp(-ENVELOPE * square)
     sine, cosine = jnp.sin(phase), jnp.cos(phase)
-    scale = -1.0 / (BOX * BOX)
-    gains[0] = scale * fade * (AMP_SIN * sine + AMP_COS * cosine)
-    gains[1] = scale * fade * (AMP_SIN * cosine - AMP_COS * sine)
-    gains[2] = fade * cosine
-    gains[3] = fade * sine
-
-    loads[5].wait()
+    gains = jnp.concatenate(
+        [
+            -fade * (AMP_SIN * sine + AMP_COS * cosine),
+            -fade * (AMP_SIN * cosine - AMP_COS * sine),
+            fade * cosine,
+            fade * sine,
+        ],
+        axis=0,
+    )
+    gh, gl = split(gains * (1.0 / BOX))
+    loads[0].wait()
+    found = dot(jnp.concatenate([gh, gl, gh], axis=1), table[...])
+    for k in range(8):
+        taps[pl.ds(k, 4 * PART, stride=8), :] = pltpu.roll(found, k, 1) if k else found
+
+    loads[2].wait()
     for g in range(BINS):
         staged[g * rows:(g + 1) * rows, :] = proj[g].astype(F32)
     for r in range(pairs):
@@ -150,30 +150,30 @@
         odd = staged[pl.ds(2 * r + 1, BINS, stride=rows), :]
         refs[q, r] = jnp.concatenate([even, odd], axis=0).astype(BF16)
 
+    def circulant(index, count, shift):
+        eight = taps[pl.ds(pl.multiple_of(index * 8, 8), 8), :]
+        return [pltpu.roll(eight, lax.rem(shift + 8 * k, BOX), 1) for k in range(count // 8)]
+
     def filter_one(p):
-        t = dot(imgs[p], h_right[...])
-        th, tl = split(t[:, :BOX] + t[:, BOX:])
-        s = dot(h_left[...], jnp.concatenate([th, tl, th], axis=0))
-        start = lax.rem(slab * rows - offs[0, p] + 2 * BOX, BOX)
-        a = h_rows[pl.ds(start, rows), :]
-        lh, ll = split(jnp.concatenate([a * gains[0, pl.ds(p, 1), :], a * gains[1, pl.ds(p, 1), :]], axis=1))
-        rh, rl = split(jnp.concatenate([s * gains[2, pl.ds(p, 1), :], s * gains[3, pl.ds(p, 1), :]], axis=0))
-        spec[pl.ds(pl.multiple_of(p * rows, rows), rows), :] = dot(lh, rh) + dot(lh, rl) + dot(ll, rh)
+        down = lax.rem(slab * rows - offs[0, p] + 2 * BOX, BOX)
+        along = lax.rem(offs[1, p] + BOX, BOX)
+        left = jnp.concatenate(circulant(p, rows, down) + circulant(PART + p, rows, down), axis=0)
+        t = dot(jnp.concatenate(split(left), axis=0), imgs[p])
+        t = t[:2 * rows] + t[2 * rows:]
+        t = jnp.concatenate([t[:rows], t[rows:]], axis=1)
+        right = circulant(2 * PART + p, BOX, along) + circulant(3 * PART + p, BOX, along)
+        right = jnp.concatenate(right, axis=0)
+        out = dot(jnp.concatenate(split(t), axis=0), jnp.concatenate(split(right), axis=1))
+        out = out[:, :BOX] + out[:, BOX:]
+        staged[pl.ds(pl.multiple_of(p * rows, rows), rows), :] = out[:rows] + out[rows:]
 
     def filter_some(step, carry):
-        for k in range(4):
-            filter_one(step * 4 + k)
+        for k in range(8):
+            filter_one(step * 8 + k)
         return carry
 
-    for load in loads[:4]:
-        load.wait()
-    lax.fori_loop(0, PART // 4, filter_some, 0)
-    loads[4].wait()
-    qh, ql = split(spec[...])
-    plain = dot(jnp.concatenate([qh, ql, qh], axis=1), h_last[...])
-    for p in range(PART):
-        shift = lax.rem(offs[1, p] + BOX, BOX)
-        staged[p * rows:(p + 1) * rows, :] = pltpu.roll(plain[p * rows:(p + 1) * rows, :], shift, 1)
+    loads[1].wait()
+    lax.fori_loop(0, PART // 8, filter_some, 0)
     for r in range(rows):
         frames[z, r] = staged[pl.ds(r, PART, stride=rows), :].astype(BF16)
 
@@ -488,12 +488,8 @@
     scratch = [
         pltpu.VMEM((PART, BOX, BOX), BF16),
         pltpu.VMEM((BINS, rows, BOX), BF16),
-        pltpu.VMEM((BOX, 2 * BOX), BF16),
-        pltpu.VMEM((BOX, 3 * BOX), BF16),
         pltpu.VMEM((3 * BOX, BOX), BF16),
-        pltpu.VMEM((BOX + rows, BOX), F32),
-        pltpu.VMEM((4, PART, BOX), F32),
-        pltpu.VMEM((PART * rows, BOX), F32),
+        pltpu.VMEM((4 * PART * 8, BOX), F32),
         pltpu.VMEM((PART * rows, BOX), F32),
         pltpu.VMEM((nz, rows, PART, BOX), BF16),
         pltpu.VMEM((nq, pairs, 2 * BINS, BOX), BF16),
@@ -514,20 +510,20 @@
         pltpu.VMEM((nz, rows, BOX), BF16),
         pltpu.VMEM((nz, rows, BOX), BF16),
     ]
-    scratch.append(dma((6,)))
+    scratch.append(dma((3,)))
     steps = PIECES * (nz - 1) // 2
     for count in (nq, nq, nz, steps, steps, ns, nz, ny, ny, ny, ny, nz, nz):
         scratch += [dma((count,)), dma((count,))]
     return pl.pallas_call(
         functools.partial(kernel, nz, nq, ns),
         out_shape=jax.ShapeDtypeStruct((2, rows, BOX), F32),
-        in_specs=[pl.BlockSpec(memory_space=pltpu.SMEM)] * 5 + [pl.BlockSpec(memory_space=pl.ANY)] * 6,
+        in_specs=[pl.BlockSpec(memory_space=pltpu.SMEM)] * 5 + [pl.BlockSpec(memory_space=pl.ANY)] * 3,
         out_specs=vmem,
         scratch_shapes=scratch,
         compiler_params=pltpu.CompilerParams(
             collective_id=0, has_side_effects=True, vmem_limit_bytes=60 * 1024 * 1024
         ),
-    )(regions, offsets, defocus, counts, tilt_angle, images, projections, *(jnp.asarray(table) for table in tables(rows)))
+    )(regions.T, offsets, defocus, counts, tilt_angle, images, projections, jnp.asarray(cosine_table()))
 
 
 def solution(mesh):

time: 70.1 us -> 64.3 us (0.917)
  Pallas kernels: 67.1 us -> 62.7 us
  local copies, waits for them, and re-layouts: 2.73 us -> 1.38 us
    pallas_call x1, Pallas kernels: 67.1 us -> 62.7 us  [body(): pl.pallas_call(functools.partial(kernel, nz, nq, ns), out_shape=jax.Shape...]
    unnamed x2 -> x1, local copies, waits for them, and re-layouts: 2.73 us -> 1.38 us
where the time goes in v2:
time: 64.3 us; the launch traced here: 64.1 us
  Pallas kernels  62.7 us (98%)
  local copies, waits for them, and re-layouts  1.38 us (2%)
    pallas_call x1, Pallas kernels, body(): pl.pallas_call(functools.partial(kernel, nz, nq, ns), out_shape=jax.Shape...  62.7 us
    unnamed x1, local copies, waits for them, and re-layouts  1.38 us

profile of v2, /device:TPU:1, one launch (start us, length us, event | category | flops | bytes accessed | tf_op | source)
XLA Modules:
  0.0 64.1 jit_solution(2204564744623344275)
XLA Ops:
  0.0 62.7 %shard_map.82 = f32[2,32,128]{2,1,0:T(8,128)} custom-call(s32[2,16]{1,0:T(2,128)} %bitcast.1, s32[2,16]{1,0:T(2,128)} %offs.1, f32[16]{0:T(128)} %defocus.1, s32[8]{0:T(128)} %counts.1, f32[8]{0:T(128)} %tilt.1, bf16[16,128,128]{2,1,0:T(8,128)(2,1)} %images_hbm.1, bf16[8,128,128]{2,1,0:T(8,128)(2,1)} %proj_hbm.1, bf16[384,128]{1,0:T(8,128)(2,1)} %constant.2.clone.table_hbm), custom_call_target="tpu_custom_call" | custom-call | tf_op jit(solution)/shard_map/pallas_call | solution.py:517
  62.8 1.4 %copy.10 = f32[2,32,128]{2,1,0:T(8,128)} copy(f32[2,32,128]{2,1,0:T(8,128)} %shard_map.82) | data formatting | bytes 65536

commit v3 on v2

--- a/solution.py
+++ b/solution.py
@@ -335,38 +335,59 @@
         share[1, :, r] = a[:, 1]
         return carry
 
-    lax.fori_loop(0, rows, average, 0, unroll=8)
-
-    def to_core(k):
+    half = rows // 2
+
+    def to_core(k, h):
         place = at_y(k)[0]
-        return pltpu.make_async_remote_copy(
-            share.at[1 - core, place], from_core.at[place], s_rc.at[k], r_rc.at[k],
+        part = pl.ds(h * half, half)
+        return pltpu.make_async_remote_copy(
+            share.at[1 - core, place, part], from_core.at[place, part], s_rc.at[2 * k + h], r_rc.at[2 * k + h],
             device_id=other_core, device_id_type=MESH,
         )
 
-    def to_owner(k):
-        return pltpu.make_async_remote_copy(
-            send_y.at[k], from_y.at[k], s_ry.at[k], r_ry.at[k], device_id=at_y(k)[1], device_id_type=MESH
+    def to_owner(k, h):
+        part = pl.ds(h * half // 2, half // 2)
+        return pltpu.make_async_remote_copy(
+            send_y.at[k, part], from_y.at[k, part], s_ry.at[2 * k + h], r_ry.at[2 * k + h],
+            device_id=at_y(k)[1], device_id_type=MESH,
+        )
+
+    span = BINS * BOX
+    mine = pl.multiple_of(q * span, span)
+
+    def block_of(place, which):
+        return pl.multiple_of((2 * place + which) * span, span)
+
+    def along_y(k, h):
+        ref = aver.at[pl.ds(h * half, half), pl.ds(mine, span)]
+        return pltpu.make_async_remote_copy(
+            ref, ref, s_ay.at[2 * k + h], r_ay.at[2 * k + h], device_id=at_y(k)[1], device_id_type=MESH
+        )
+
+    def across(k, h):
+        ref = aver.at[pl.ds(h * half, half), pl.ds(block_of(lax.rem(y - k + ny, ny), core), span)]
+        return pltpu.make_async_remote_copy(
+            ref, ref, s_ac.at[2 * k + h], r_ac.at[2 * k + h], device_id=other_core, device_id_type=MESH
         )
 
     far_first = sorted(range(1, ny), key=lambda k: -min(k, ny - k))
-    for k in far_first + [0]:
-        to_core(k).start()
-    for k in far_first:
-        place = at_y(k)[0]
-        to_core(k).wait_recv()
-
-        def pack(r, carry):
-            a = share[core, place, 2 * r] + from_core[place, 2 * r]
-            b = share[core, place, 2 * r + 1] + from_core[place, 2 * r + 1]
-            send_y[k, r] = jnp.concatenate([a, b], axis=0).astype(BF16)
-            return carry
-
-        lax.fori_loop(0, pairs, pack, 0, unroll=8)
-        to_owner(k).start()
-    to_core(0).wait_recv()
-    for k in range(1, ny):
-        to_owner(k).wait_recv()
+    for h in range(2):
+        lax.fori_loop(h * half, (h + 1) * half, average, 0, unroll=8)
+        for k in far_first + [0]:
+            to_core(k, h).start()
+    for h in range(2):
+        for k in far_first:
+            place = at_y(k)[0]
+            to_core(k, h).wait_recv()
+
+            def pack(r, carry):
+                a = share[core, place, 2 * r] + from_core[place, 2 * r]
+                b = share[core, place, 2 * r + 1] + from_core[place, 2 * r + 1]
+                send_y[k, r] = jnp.concatenate([a, b], axis=0).astype(BF16)
+                return carry
+
+            lax.fori_loop(h * half // 2, (h + 1) * half // 2, pack, 0, unroll=8)
+            to_owner(k, h).start()
 
     def add_up(r, carry):
         a = share[core, y, 2 * r] + from_core[y, 2 * r]
@@ -377,27 +398,17 @@
         total[pl.ds(pl.multiple_of(r * 2 * BINS, 2 * BINS), 2 * BINS), :] = value
         return carry
 
-    lax.fori_loop(0, pairs, add_up, 0, unroll=8)
-    span = BINS * BOX
-    mine = pl.multiple_of(q * span, span)
-    for g in range(BINS):
-        block = total[pl.ds(g, rows, stride=BINS), :].astype(BF16)
-        aver[0:rows, pl.ds(pl.multiple_of(mine + g * BOX, BOX), BOX)] = block
-
-    def block_of(place, which):
-        return pl.multiple_of((2 * place + which) * span, span)
-
-    def along_y(k):
-        ref = aver.at[pl.ds(0, rows), pl.ds(mine, span)]
-        return pltpu.make_async_remote_copy(ref, ref, s_ay.at[k], r_ay.at[k], device_id=at_y(k)[1], device_id_type=MESH)
-
-    def across(k):
-        ref = aver.at[pl.ds(0, rows), pl.ds(block_of(lax.rem(y - k + ny, ny), core), span)]
-        return pltpu.make_async_remote_copy(ref, ref, s_ac.at[k], r_ac.at[k], device_id=other_core, device_id_type=MESH)
-
-    for k in far_first:
-        along_y(k).start()
-    across(0).start()
+    for h in range(2):
+        to_core(0, h).wait_recv()
+        for k in far_first[::-1]:
+            to_owner(k, h).wait_recv()
+        lax.fori_loop(h * half // 2, (h + 1) * half // 2, add_up, 0, unroll=8)
+        for g in range(BINS):
+            block = total[pl.ds(h * half * BINS + g, half, stride=BINS), :].astype(BF16)
+            aver[h * half:(h + 1) * half, pl.ds(pl.multiple_of(mine + g * BOX, BOX), BOX)] = block
+        for k in far_first:
+            along_y(k, h).start()
+        across(0, h).start()
 
     mirror = (
         lax.broadcasted_iota(jnp.int32, (BOX, BOX), 0) + lax.broadcasted_iota(jnp.int32, (BOX, BOX), 1) == BOX - 1
@@ -419,18 +430,27 @@
             block = project(base, at)
             planes[:, at] = block if first else planes[:, at] + block
 
+    def back(k, which):
+        return block_of(lax.rem(y - k + ny, ny), which)
+
     near_first = far_first[::-1]
-    add_block(block_of(y, core), True)
-    across(0).wait_recv()
-    add_block(block_of(y, 1 - core), False)
+    add_block(back(0, core), True)
+    for h in range(2):
+        across(0, h).wait_recv()
+    add_block(back(0, 1 - core), False)
     for k in near_first:
-        along_y(k).wait_recv()
-        across(k).start()
-        add_block(block_of(lax.rem(y - k + ny, ny), core), False)
-        across(k).wait_recv()
+        along_y(k, 0).wait_recv()
+        across(k, 0).start()
+    for k in near_first:
+        along_y(k, 1).wait_recv()
+        across(k, 1).start()
+        add_block(back(k, core), False)
+    for k in near_first:
+        for h in range(2):
+            across(k, h).wait_recv()
         if k != near_first[-1]:
-            add_block(block_of(lax.rem(y - k + ny, ny), 1 - core), False)
-    final = block_of(lax.rem(y - near_first[-1] + ny, ny), 1 - core)
+            add_block(back(k, 1 - core), False)
+    final = back(near_first[-1], 1 - core)
     reverse(final)
 
     def even_copy(k):
@@ -461,11 +481,12 @@
         if k:
             even_copy(k).wait()
     for k in range(ny):
-        to_core(k).wait_send()
-        across(k).wait_send()
-        if k:
-            to_owner(k).wait_send()
-            along_y(k).wait_send()
+        for h in range(2):
+            to_core(k, h).wait_send()
+            across(k, h).wait_send()
+            if k:
+                to_owner(k, h).wait_send()
+                along_y(k, h).wait_send()
     value = give_e[0].astype(F32)
     for k in range(1, nz):
         value = value + take_e[k].astype(F32)
@@ -512,11 +533,11 @@
     ]
     scratch.append(dma((3,)))
     steps = PIECES * (nz - 1) // 2
-    for count in (nq, nq, nz, steps, steps, ns, nz, ny, ny, ny, ny, nz, nz):
+    for count in (nq, nq, nz, steps, steps, ns, nz, 2 * ny, 2 * ny, 2 * ny, 2 * ny, nz, nz):
         scratch += [dma((count,)), dma((count,))]
     return pl.pallas_call(
         functools.partial(kernel, nz, nq, ns),
-        out_shape=jax.ShapeDtypeStruct((2, rows, BOX), F32),
+        out_shape=pltpu.VMEM((2, rows, BOX), F32),
         in_specs=[pl.BlockSpec(memory_space=pltpu.SMEM)] * 5 + [pl.BlockSpec(memory_space=pl.ANY)] * 3,
         out_specs=vmem,
         scratch_shapes=scratch,

time: 64.3 us -> 60.6 us (0.942)
  Pallas kernels: 62.7 us -> 59.9 us
  local copies, waits for them, and re-layouts: 1.38 us -> 0.62 us
    pallas_call x1, Pallas kernels: 62.7 us -> 59.9 us  [body(): pl.pallas_call(functools.partial(kernel, nz, nq, ns), out_shape=pltpu.VME...]
    unnamed x1, local copies, waits for them, and re-layouts: 1.38 us -> 0.62 us
where the time goes in v3:
time: 60.6 us; the launch traced here: 60.5 us
  Pallas kernels  59.9 us (99%)
  local copies, waits for them, and re-layouts  0.62 us (1%)
    pallas_call x1, Pallas kernels, body(): pl.pallas_call(functools.partial(kernel, nz, nq, ns), out_shape=pltpu.VME...  59.9 us

profile of v3, /device:TPU:1, one launch (start us, length us, event | category | flops | bytes accessed | tf_op | source)
XLA Modules:
  0.0 60.5 jit_solution(6098574494656195885)
XLA Ops:
  0.0 59.9 %shard_map.82 = f32[2,32,128]{2,1,0:T(8,128)S(1)} custom-call(s32[2,16]{1,0:T(2,128)} %bitcast.1, s32[2,16]{1,0:T(2,128)} %offs.1, f32[16]{0:T(128)} %defocus.1, s32[8]{0:T(128)} %counts.1, f32[8]{0:T(128)} %tilt.1, bf16[16,128,128]{2,1,0:T(8,128)(2,1)} %images_hbm.1, bf16[8,128,128]{2,1,0:T(8,128)(2,1)} %proj_hbm.1, bf16[384,128]{1,0:T(8,128)(2,1)} %constant.2.clone.table_hbm), custom_call_target="tpu_custom_call" | custom-call | tf_op jit(solution)/shard_map/pallas_call | solution.py:538
  59.9 0.6 %copy.10 = f32[2,32,128]{2,1,0:T(8,128)} copy(f32[2,32,128]{2,1,0:T(8,128)S(1)} %shard_map.82) | data formatting | bytes 65536

commit v4 on v3

--- a/solution.py
+++ b/solution.py
@@ -145,10 +145,10 @@
     loads[2].wait()
     for g in range(BINS):
         staged[g * rows:(g + 1) * rows, :] = proj[g].astype(F32)
-    for r in range(pairs):
-        even = staged[pl.ds(2 * r, BINS, stride=rows), :]
-        odd = staged[pl.ds(2 * r + 1, BINS, stride=rows), :]
-        refs[q, r] = jnp.concatenate([even, odd], axis=0).astype(BF16)
+    for r in range(rows // 4):
+        lines = [staged[pl.ds(4 * r + k, BINS, stride=rows), :] for k in range(4)]
+        upper, lower = jnp.concatenate(lines[:2], axis=1), jnp.concatenate(lines[2:], axis=1)
+        refs[q, r] = jnp.concatenate([upper, lower], axis=0).astype(BF16)
 
     def circulant(index, count, shift):
         eight = taps[pl.ds(pl.multiple_of(index * 8, 8), 8), :]
@@ -242,8 +242,6 @@
         left(step).wait_recv()
         if step + PIECES < steps:
             left(step + PIECES).start()
-        for unit in range(step * units // steps, (step + 1) * units // steps):
-            weigh(unit)
 
     for k in range(1, nq):
         to_q(refs, s_pr, r_pr, k).wait()
@@ -258,16 +256,16 @@
     def frame(r):
         return frames[:, r].reshape(lanes, BOX)
 
-    def score(r, carry):
-        even, odd = carry
-        a = refs[:, r].reshape(nq * 2 * BINS, BOX)
-        return even + dot_nt(a, frame(2 * r)), odd + dot_nt(a, frame(2 * r + 1))
-
-    zero = jnp.zeros((nq * 2 * BINS, lanes), F32)
-    even, odd = lax.fori_loop(0, pairs, score, (zero, zero), unroll=4)
-    even = even.reshape(nq, 2, BINS, lanes)[:, 0]
-    odd = odd.reshape(nq, 2, BINS, lanes)[:, 1]
-    scores = even + odd
+    def frame_pair(r):
+        return jnp.concatenate([frame(2 * r), frame(2 * r + 1)], axis=1)
+
+    def score(r, found):
+        a = refs[:, r].reshape(nq * 2 * BINS, 2 * BOX)
+        return found + dot_nt(a, jnp.concatenate([frame_pair(2 * r), frame_pair(2 * r + 1)], axis=0))
+
+    found = jnp.zeros((nq * 2 * BINS, 2 * lanes), F32)
+    found = lax.fori_loop(0, rows // 4, score, found, unroll=4).reshape(nq, 2, BINS, 2 * lanes)
+    scores = found[:, 0, :, :lanes] + found[:, 1, :, lanes:]
 
     named = meta_z[0]
     for k in range(1, nz):
@@ -293,6 +291,8 @@
 
     for k in range(1, ns):
         to_x(k).start()
+    for unit in range(units // 3):
+        weigh(unit)
     for k in range(1, ns):
         to_x(k).wait()
     scores = partial[0]
@@ -310,6 +310,8 @@
     stats[z, 1:2, :lanes] = summed
     for k in range(1, nz):
         to_z(stats, s_st, r_st, k).start()
+    for unit in range(units // 3, units):
+        weigh(unit)
     for k in range(1, nz):
         to_z(stats, s_st, r_st, k).wait()
     best = stats[0, 0:1, :lanes]
@@ -330,9 +332,10 @@
     posterior = jnp.concatenate(posterior, axis=0).astype(BF16)
 
     def average(r, carry):
-        a = dot(posterior, frame(r)).reshape(ny, 2, BINS, BOX)
-        share[0, :, r] = a[:, 0]
-        share[1, :, r] = a[:, 1]
+        a = dot(posterior, frame_pair(r)).reshape(ny, 2, BINS, 2 * BOX)
+        for which in range(2):
+            share[which, :, 2 * r] = a[:, which, :, :BOX]
+            share[which, :, 2 * r + 1] = a[:, which, :, BOX:]
         return carry
 
     half = rows // 2
@@ -372,7 +375,7 @@
 
     far_first = sorted(range(1, ny), key=lambda k: -min(k, ny - k))
     for h in range(2):
-        lax.fori_loop(h * half, (h + 1) * half, average, 0, unroll=8)
+        lax.fori_loop(h * half // 2, (h + 1) * half // 2, average, 0, unroll=8)
         for k in far_first + [0]:
             to_core(k, h).start()
     for h in range(2):
@@ -414,17 +417,18 @@
         lax.broadcasted_iota(jnp.int32, (BOX, BOX), 0) + lax.broadcasted_iota(jnp.int32, (BOX, BOX), 1) == BOX - 1
     ).astype(F32).astype(BF16)
 
-    def reverse(base):
-        tiles = [aver[0:rows, pl.ds(pl.multiple_of(base + g * BOX, BOX), BOX)] for g in range(BINS)]
+    def reverse(base, h):
+        part = slice(h * half, (h + 1) * half)
+        tiles = [aver[part, pl.ds(pl.multiple_of(base + g * BOX, BOX), BOX)] for g in range(BINS)]
         turned = dot(jnp.concatenate(tiles, axis=0), mirror).astype(BF16)
+        part = slice(rows + h * half, rows + (h + 1) * half)
         for g in range(BINS):
-            aver[rows:2 * rows, pl.ds(pl.multiple_of(base + g * BOX, BOX), BOX)] = turned[g * rows:(g + 1) * rows]
+            aver[part, pl.ds(pl.multiple_of(base + g * BOX, BOX), BOX)] = turned[g * half:(g + 1) * half]
 
     def project(base, lanes_at):
         return dot(aver[:, pl.ds(base, span)], weights[pl.ds(base, span), lanes_at])
 
     def add_block(base, first):
-        reverse(base)
         for pair in range(nz // 2):
             at = slice(2 * pair * BOX, (2 * pair + 2) * BOX)
             block = project(base, at)
@@ -434,24 +438,30 @@
         return block_of(lax.rem(y - k + ny, ny), which)
 
     near_first = far_first[::-1]
+    for h in range(2):
+        reverse(back(0, core), h)
     add_block(back(0, core), True)
     for h in range(2):
         across(0, h).wait_recv()
+        reverse(back(0, 1 - core), h)
     add_block(back(0, 1 - core), False)
     for k in near_first:
         along_y(k, 0).wait_recv()
         across(k, 0).start()
+        reverse(back(k, core), 0)
     for k in near_first:
         along_y(k, 1).wait_recv()
         across(k, 1).start()
+        reverse(back(k, core), 1)
         add_block(back(k, core), False)
+        across(k, 0).wait_recv()
+        reverse(back(k, 1 - core), 0)
     for k in near_first:
-        for h in range(2):
-            across(k, h).wait_recv()
+        across(k, 1).wait_recv()
+        reverse(back(k, 1 - core), 1)
         if k != near_first[-1]:
             add_block(back(k, 1 - core), False)
     final = back(near_first[-1], 1 - core)
-    reverse(final)
 
     def even_copy(k):
         return pltpu.make_async_remote_copy(
@@ -513,7 +523,7 @@
         pltpu.VMEM((4 * PART * 8, BOX), F32),
         pltpu.VMEM((PART * rows, BOX), F32),
         pltpu.VMEM((nz, rows, PART, BOX), BF16),
-        pltpu.VMEM((nq, pairs, 2 * BINS, BOX), BF16),
+        pltpu.VMEM((nq, rows // 4, 2 * BINS, 2 * BOX), BF16),
         pltpu.VMEM((nq, 24, BOX), F32),
         pltpu.VMEM((nz, 8, BOX), jnp.int32),
         pltpu.VMEM((ns, 2 * BINS, nz * PART), F32),

time: 60.6 us -> 59.7 us (0.985)
  Pallas kernels: 59.9 us -> 59 us
    pallas_call x1, Pallas kernels: 59.9 us -> 59 us  [body(): pl.pallas_call(functools.partial(kernel, nz, nq, ns), out_shape=pltpu.VME...]
where the time goes in v4:
time: 59.7 us; the launch traced here: 59.6 us
  Pallas kernels  59 us (99%)
  local copies, waits for them, and re-layouts  0.62 us (1%)
    pallas_call x1, Pallas kernels, body(): pl.pallas_call(functools.partial(kernel, nz, nq, ns), out_shape=pltpu.VME...  59 us

profile of v4, /device:TPU:1, one launch (start us, length us, event | category | flops | bytes accessed | tf_op | source)
XLA Modules:
  0.0 59.6 jit_solution(17332991396593908429)
XLA Ops:
  0.0 59.0 %shard_map.82 = f32[2,32,128]{2,1,0:T(8,128)S(1)} custom-call(s32[2,16]{1,0:T(2,128)} %bitcast.1, s32[2,16]{1,0:T(2,128)} %offs.1, f32[16]{0:T(128)} %defocus.1, s32[8]{0:T(128)} %counts.1, f32[8]{0:T(128)} %tilt.1, bf16[16,128,128]{2,1,0:T(8,128)(2,1)} %images_hbm.1, bf16[8,128,128]{2,1,0:T(8,128)(2,1)} %proj_hbm.1, bf16[384,128]{1,0:T(8,128)(2,1)} %constant.2.clone.table_hbm), custom_call_target="tpu_custom_call" | custom-call | tf_op jit(solution)/shard_map/pallas_call | solution.py:548
  59.0 0.6 %copy.10 = f32[2,32,128]{2,1,0:T(8,128)} copy(f32[2,32,128]{2,1,0:T(8,128)S(1)} %shard_map.82) | data formatting | bytes 65536

commit v5 on v4

--- a/solution.py
+++ b/solution.py
@@ -211,7 +211,7 @@
     for k in range(1, nq):
         to_q(refs, s_pr, r_pr, k).start()
     for k in range(1, nq):
-        to_q(meta_p, s_mp, r_mp, k).wait()
+        to_q(meta_p, s_mp, r_mp, k).wait_recv()
 
     column = lax.broadcasted_iota(jnp.int32, (1, BOX), 1).astype(F32) - centre
     height = lax.broadcasted_iota(jnp.int32, (BOX, BOX), 0).astype(F32)
@@ -244,12 +244,9 @@
             left(step + PIECES).start()
 
     for k in range(1, nq):
-        to_q(refs, s_pr, r_pr, k).wait()
-    for k in range(1, nz):
-        to_z(meta_z, s_mz, r_mz, k).wait()
-    for step in range(steps):
-        right(step).wait_send()
-        left(step).wait_send()
+        to_q(refs, s_pr, r_pr, k).wait_recv()
+    for k in range(1, nz):
+        to_z(meta_z, s_mz, r_mz, k).wait_recv()
 
     lanes = nz * PART
 
@@ -294,7 +291,7 @@
     for unit in range(units // 3):
         weigh(unit)
     for k in range(1, ns):
-        to_x(k).wait()
+        to_x(k).wait_recv()
     scores = partial[0]
     for k in range(1, ns):
         scores = scores + partial[k]
@@ -312,8 +309,17 @@
         to_z(stats, s_st, r_st, k).start()
     for unit in range(units // 3, units):
         weigh(unit)
-    for k in range(1, nz):
-        to_z(stats, s_st, r_st, k).wait()
+    for step in range(steps):
+        right(step).wait_send()
+        left(step).wait_send()
+    for k in range(1, nq):
+        to_q(meta_p, s_mp, r_mp, k).wait_send()
+        to_q(refs, s_pr, r_pr, k).wait_send()
+    for k in range(1, ns):
+        to_x(k).wait_send()
+    for k in range(1, nz):
+        to_z(meta_z, s_mz, r_mz, k).wait_send()
+        to_z(stats, s_st, r_st, k).wait_recv()
     best = stats[0, 0:1, :lanes]
     for k in range(1, nz):
         best = jnp.maximum(best, stats[k, 0:1, :lanes])
@@ -486,10 +492,8 @@
             if k:
                 even_copy(k).start()
 
-    for k in range(nz):
-        odd_copy(k).wait()
-        if k:
-            even_copy(k).wait()
+    for k in range(1, nz):
+        to_z(stats, s_st, r_st, k).wait_send()
     for k in range(ny):
         for h in range(2):
             to_core(k, h).wait_send()
@@ -497,17 +501,20 @@
             if k:
                 to_owner(k, h).wait_send()
                 along_y(k, h).wait_send()
+    for k in range(nz):
+        odd_copy(k).wait_send()
+        if k:
+            even_copy(k).wait_send()
     value = give_e[0].astype(F32)
-    for k in range(1, nz):
+    for k in sorted(range(1, nz), key=lambda k: min(k, nz - k)):
+        even_copy(k).wait_recv()
         value = value + take_e[k].astype(F32)
     out[0] = value
-    value = take_o[0].astype(F32)
-    for k in range(1, nz):
-        value = value + take_o[k].astype(F32)
-    high, rest = split(value)
-    middle = (value - high.astype(F32)).astype(BF16)
-    lowest = (value - high.astype(F32) - middle.astype(F32)).astype(BF16)
-    out[1] = dot(jnp.concatenate([high, middle, lowest], axis=1), jnp.concatenate([mirror] * 3, axis=0))
+    for k in range(nz):
+        odd_copy(k).wait_recv()
+    out[1] = dot(
+        jnp.concatenate([take_o[k] for k in range(nz)], axis=1), jnp.concatenate([mirror] * nz, axis=0)
+    )
 
 
 def body(nz, nq, ns, images, projections, regions, offsets, defocus, counts, tilt_angle):

time: 59.7 us -> 59.2 us (level)
  no operation moved by 1% of the time
where the time goes in v5:
time: 59.2 us; the launch traced here: 59.1 us
  Pallas kernels  58.5 us (99%)
  local copies, waits for them, and re-layouts  0.62 us (1%)
    pallas_call x1, Pallas kernels, body(): pl.pallas_call(functools.partial(kernel, nz, nq, ns), out_shape=pltpu.VME...  58.5 us

profile of v5, /device:TPU:1, one launch (start us, length us, event | category | flops | bytes accessed | tf_op | source)
XLA Modules:
  0.0 59.1 jit_solution(660241641195335580)
XLA Ops:
  0.0 58.5 %shard_map.82 = f32[2,32,128]{2,1,0:T(8,128)S(1)} custom-call(s32[2,16]{1,0:T(2,128)} %bitcast.1, s32[2,16]{1,0:T(2,128)} %offs.1, f32[16]{0:T(128)} %defocus.1, s32[8]{0:T(128)} %counts.1, f32[8]{0:T(128)} %tilt.1, bf16[16,128,128]{2,1,0:T(8,128)(2,1)} %images_hbm.1, bf16[8,128,128]{2,1,0:T(8,128)(2,1)} %proj_hbm.1, bf16[384,128]{1,0:T(8,128)(2,1)} %constant.2.clone.table_hbm), custom_call_target="tpu_custom_call" | custom-call | tf_op jit(solution)/shard_map/pallas_call | solution.py:555
  58.5 0.6 %copy.10 = f32[2,32,128]{2,1,0:T(8,128)} copy(f32[2,32,128]{2,1,0:T(8,128)S(1)} %shard_map.82) | data formatting | bytes 65536

commit v6 on v5

--- a/solution.py
+++ b/solution.py
@@ -62,9 +62,10 @@
     slab = lax.axis_index("slab")
     z = me // nq
     q = lax.rem(me, nq)
-    flip_q = nq - 1 - q
     y = q // 2
     core = lax.rem(q, 2)
+    mate = q + 1 - 2 * core
+    flip_q = nq - 1 - mate
     other_core = (z * nq + 2 * y + 1 - core, slab)
     centre = (BOX - 1) / 2.0
 
@@ -96,26 +97,10 @@
 
     barrier = pltpu.get_barrier_semaphore()
     partners = [at_q(k)[1] for k in range(1, nq)] + [at_z(k)[1] for k in range(1, nz)]
-    partners += [(lax.rem(z + k, nz) * nq + flip_q, slab) for k in range(1, nz)]
+    partners += [(lax.rem(z + k, nz) * nq + other, slab) for k in range(1, nz) for other in (mate, flip_q)]
     partners += [(me, lax.rem(slab + k, ns)) for k in range(1, ns)]
     for device in partners:
         pl.semaphore_signal(barrier, inc=1, device_id=device, device_id_type=MESH)
-
-    lane = lax.broadcasted_iota(jnp.int32, (8, BOX), 1)
-    line = lax.broadcasted_iota(jnp.int32, (8, BOX), 0)
-    angle = jnp.zeros((8, BOX), F32)
-    count = jnp.zeros((8, BOX), jnp.int32)
-    for g in range(BINS):
-        angle = jnp.where(line == g, tilt[g], angle)
-        count = jnp.where(line == g, counts[g], count)
-    meta_p[q, 0:8, :] = jnp.log(1.0 + count.astype(F32))
-    meta_p[q, 8:16, :] = jnp.cos(angle)
-    meta_p[q, 16:24, :] = jnp.sin(angle)
-    named = jnp.zeros((8, BOX), jnp.int32)
-    for p in range(PART):
-        for t in range(2):
-            named = jnp.where((lane == z * PART + p) & (line == t), regions[t, p], named)
-    meta_z[z] = named
 
     index = lax.broadcasted_iota(jnp.int32, (PART, BOX), 1)
     which = lax.broadcasted_iota(jnp.int32, (PART, BOX), 0)
@@ -142,14 +127,6 @@
     for k in range(8):
         taps[pl.ds(k, 4 * PART, stride=8), :] = pltpu.roll(found, k, 1) if k else found
 
-    loads[2].wait()
-    for g in range(BINS):
-        staged[g * rows:(g + 1) * rows, :] = proj[g].astype(F32)
-    for r in range(rows // 4):
-        lines = [staged[pl.ds(4 * r + k, BINS, stride=rows), :] for k in range(4)]
-        upper, lower = jnp.concatenate(lines[:2], axis=1), jnp.concatenate(lines[2:], axis=1)
-        refs[q, r] = jnp.concatenate([upper, lower], axis=0).astype(BF16)
-
     def circulant(index, count, shift):
         eight = taps[pl.ds(pl.multiple_of(index * 8, 8), 8), :]
         return [pltpu.roll(eight, lax.rem(shift + 8 * k, BOX), 1) for k in range(count // 8)]
@@ -168,12 +145,12 @@
         staged[pl.ds(pl.multiple_of(p * rows, rows), rows), :] = out[:rows] + out[rows:]
 
     def filter_some(step, carry):
-        for k in range(8):
-            filter_one(step * 8 + k)
+        for k in range(16):
+            filter_one(step * 16 + k)
         return carry
 
     loads[1].wait()
-    lax.fori_loop(0, PART // 8, filter_some, 0)
+    lax.fori_loop(0, PART // 16, filter_some, 0)
     for r in range(rows):
         frames[z, r] = staged[pl.ds(r, PART, stride=rows), :].astype(BF16)
 
@@ -204,10 +181,34 @@
     for step in range(PIECES):
         right(step).start()
         left(step).start()
+
+    lane = lax.broadcasted_iota(jnp.int32, (8, BOX), 1)
+    line = lax.broadcasted_iota(jnp.int32, (8, BOX), 0)
+    angle = jnp.zeros((8, BOX), F32)
+    count = jnp.zeros((8, BOX), jnp.int32)
+    for g in range(BINS):
+        angle = jnp.where(line == g, tilt[g], angle)
+        count = jnp.where(line == g, counts[g], count)
+    meta_p[q, 0:8, :] = jnp.log(1.0 + count.astype(F32))
+    meta_p[q, 8:16, :] = jnp.cos(angle)
+    meta_p[q, 16:24, :] = jnp.sin(angle)
+    named = jnp.zeros((8, BOX), jnp.int32)
+    for p in range(PART):
+        for t in range(2):
+            named = jnp.where((lane == z * PART + p) & (line == t), regions[t, p], named)
+    meta_z[z] = named
+
     for k in range(1, nq):
         to_q(meta_p, s_mp, r_mp, k).start()
     for k in range(1, nz):
         to_z(meta_z, s_mz, r_mz, k).start()
+    loads[2].wait()
+    for g in range(BINS):
+        staged[g * rows:(g + 1) * rows, :] = proj[g].astype(F32)
+    for r in range(rows // 4):
+        lines = [staged[pl.ds(4 * r + k, BINS, stride=rows), :] for k in range(4)]
+        upper, lower = jnp.concatenate(lines[:2], axis=1), jnp.concatenate(lines[2:], axis=1)
+        refs[q, r] = jnp.concatenate([upper, lower], axis=0).astype(BF16)
     for k in range(1, nq):
         to_q(refs, s_pr, r_pr, k).start()
     for k in range(1, nq):
@@ -224,7 +225,7 @@
             sinr = meta_p[j, pl.ds(16 + g, 1), :]
             base = pl.multiple_of((j * BINS + g) * BOX, BOX)
             for k in range(nz):
-                plane = 2 * (lax.rem(z + k, nz) * nq + q)
+                plane = 2 * (lax.rem(z + k, nz) * nq + mate)
                 away = plane.astype(F32) - (depth - 1) / 2.0
                 landing = column * cosr + away * sinr + centre
                 w = jnp.maximum(0.0, 1.0 - jnp.abs(landing - height))
@@ -368,13 +369,13 @@
         return pl.multiple_of((2 * place + which) * span, span)
 
     def along_y(k, h):
-        ref = aver.at[pl.ds(h * half, half), pl.ds(mine, span)]
+        ref = aver.at[pl.ds(2 * h * half, half), pl.ds(mine, span)]
         return pltpu.make_async_remote_copy(
             ref, ref, s_ay.at[2 * k + h], r_ay.at[2 * k + h], device_id=at_y(k)[1], device_id_type=MESH
         )
 
     def across(k, h):
-        ref = aver.at[pl.ds(h * half, half), pl.ds(block_of(lax.rem(y - k + ny, ny), core), span)]
+        ref = aver.at[pl.ds(2 * h * half, 2 * half), pl.ds(block_of(lax.rem(y - k + ny, ny), core), span)]
         return pltpu.make_async_remote_copy(
             ref, ref, s_ac.at[2 * k + h], r_ac.at[2 * k + h], device_id=other_core, device_id_type=MESH
         )
@@ -398,6 +399,18 @@
             lax.fori_loop(h * half // 2, (h + 1) * half // 2, pack, 0, unroll=8)
             to_owner(k, h).start()
 
+    mirror = (
+        lax.broadcasted_iota(jnp.int32, (BOX, BOX), 0) + lax.broadcasted_iota(jnp.int32, (BOX, BOX), 1) == BOX - 1
+    ).astype(F32).astype(BF16)
+
+    def reverse(base, h):
+        first = 2 * h * half
+        tiles = [aver[first:first + half, pl.ds(pl.multiple_of(base + g * BOX, BOX), BOX)] for g in range(BINS)]
+        turned = dot(jnp.concatenate(tiles, axis=0), mirror).astype(BF16)
+        for g in range(BINS):
+            at = pl.ds(pl.multiple_of(base + g * BOX, BOX), BOX)
+            aver[first + half:first + 2 * half, at] = turned[g * half:(g + 1) * half]
+
     def add_up(r, carry):
         a = share[core, y, 2 * r] + from_core[y, 2 * r]
         b = share[core, y, 2 * r + 1] + from_core[y, 2 * r + 1]
@@ -414,22 +427,11 @@
         lax.fori_loop(h * half // 2, (h + 1) * half // 2, add_up, 0, unroll=8)
         for g in range(BINS):
             block = total[pl.ds(h * half * BINS + g, half, stride=BINS), :].astype(BF16)
-            aver[h * half:(h + 1) * half, pl.ds(pl.multiple_of(mine + g * BOX, BOX), BOX)] = block
+            aver[2 * h * half:(2 * h + 1) * half, pl.ds(pl.multiple_of(mine + g * BOX, BOX), BOX)] = block
         for k in far_first:
             along_y(k, h).start()
+        reverse(mine, h)
         across(0, h).start()
-
-    mirror = (
-        lax.broadcasted_iota(jnp.int32, (BOX, BOX), 0) + lax.broadcasted_iota(jnp.int32, (BOX, BOX), 1) == BOX - 1
-    ).astype(F32).astype(BF16)
-
-    def reverse(base, h):
-        part = slice(h * half, (h + 1) * half)
-        tiles = [aver[part, pl.ds(pl.multiple_of(base + g * BOX, BOX), BOX)] for g in range(BINS)]
-        turned = dot(jnp.concatenate(tiles, axis=0), mirror).astype(BF16)
-        part = slice(rows + h * half, rows + (h + 1) * half)
-        for g in range(BINS):
-            aver[part, pl.ds(pl.multiple_of(base + g * BOX, BOX), BOX)] = turned[g * half:(g + 1) * half]
 
     def project(base, lanes_at):
         return dot(aver[:, pl.ds(base, span)], weights[pl.ds(base, span), lanes_at])
@@ -444,34 +446,30 @@
         return block_of(lax.rem(y - k + ny, ny), which)
 
     near_first = far_first[::-1]
-    for h in range(2):
-        reverse(back(0, core), h)
     add_block(back(0, core), True)
     for h in range(2):
         across(0, h).wait_recv()
-        reverse(back(0, 1 - core), h)
     add_block(back(0, 1 - core), False)
     for k in near_first:
         along_y(k, 0).wait_recv()
+        reverse(back(k, core), 0)
         across(k, 0).start()
-        reverse(back(k, core), 0)
     for k in near_first:
         along_y(k, 1).wait_recv()
+        reverse(back(k, core), 1)
         across(k, 1).start()
-        reverse(back(k, core), 1)
         add_block(back(k, core), False)
-        across(k, 0).wait_recv()
-        reverse(back(k, 1 - core), 0)
     for k in near_first:
-        across(k, 1).wait_recv()
-        reverse(back(k, 1 - core), 1)
+        for h in range(2):
+            across(k, h).wait_recv()
         if k != near_first[-1]:
             add_block(back(k, 1 - core), False)
     final = back(near_first[-1], 1 - core)
 
     def even_copy(k):
-        return pltpu.make_async_remote_copy(
-            give_e.at[k], take_e.at[k], s_e.at[k], r_e.at[k], device_id=at_z(k)[1], device_id_type=MESH
+        device = (lax.rem(z + k, nz) * nq + mate, slab)
+        return pltpu.make_async_remote_copy(
+            give_e.at[k], take_e.at[k], s_e.at[k], r_e.at[k], device_id=device, device_id_type=MESH
         )
 
     def odd_copy(k):
@@ -480,17 +478,16 @@
             give_o.at[k], take_o.at[k], s_o.at[k], r_o.at[k], device_id=device, device_id_type=MESH
         )
 
-    order = sorted(range(nz // 2), key=lambda pair: -min(2 * pair, nz - 2 * pair))
-    for pair in order:
-        at = slice(2 * pair * BOX, (2 * pair + 2) * BOX)
-        block = planes[:, at] + project(final, at)
-        for k in (2 * pair, 2 * pair + 1):
-            at = (k - 2 * pair) * BOX
-            give_e[k] = block[:rows, at:at + BOX].astype(BF16)
-            give_o[k] = block[rows:, at:at + BOX].astype(BF16)
-            odd_copy(k).start()
-            if k:
-                even_copy(k).start()
+    for turn in sorted(range(nz // 2), key=lambda turn: min(turn, nz // 2 - turn)):
+        pair = lax.rem(nz // 4 - 1 + nz + turn - z, nz // 2)
+        at = pl.ds(pl.multiple_of(2 * pair * BOX, 2 * BOX), 2 * BOX)
+        block = (planes[:, at] + project(final, at)).reshape(2, 2, half, 2 * BOX)
+        for k in range(2):
+            give_o[2 * pair + k] = block[:, 1, :, k * BOX:(k + 1) * BOX].reshape(rows, BOX).astype(BF16)
+            odd_copy(2 * pair + k).start()
+        for k in range(2):
+            give_e[2 * pair + k] = block[:, 0, :, k * BOX:(k + 1) * BOX].reshape(rows, BOX).astype(BF16)
+            even_copy(2 * pair + k).start()
 
     for k in range(1, nz):
         to_z(stats, s_st, r_st, k).wait_send()
@@ -503,10 +500,9 @@
                 along_y(k, h).wait_send()
     for k in range(nz):
         odd_copy(k).wait_send()
-        if k:
-            even_copy(k).wait_send()
-    value = give_e[0].astype(F32)
-    for k in sorted(range(1, nz), key=lambda k: min(k, nz - k)):
+        even_copy(k).wait_send()
+    value = jnp.zeros((rows, BOX), F32)
+    for k in sorted(range(nz), key=lambda k: min(k, nz - k)):
         even_copy(k).wait_recv()
         value = value + take_e[k].astype(F32)
     out[0] = value

time: 59.2 us -> 58.6 us (0.990)
  Pallas kernels: 58.5 us -> 57.9 us
    pallas_call x1, Pallas kernels: 58.5 us -> 57.9 us  [body(): pl.pallas_call(functools.partial(kernel, nz, nq, ns), out_shape=pltpu.VME...]
where the time goes in v6:
time: 58.6 us; the launch traced here: 58.5 us
  Pallas kernels  57.9 us (99%)
  local copies, waits for them, and re-layouts  0.62 us (1%)
    pallas_call x1, Pallas kernels, body(): pl.pallas_call(functools.partial(kernel, nz, nq, ns), out_shape=pltpu.VME...  57.9 us

profile of v6, /device:TPU:1, one launch (start us, length us, event | category | flops | bytes accessed | tf_op | source)
XLA Modules:
  0.0 58.5 jit_solution(13997655555499354688)
XLA Ops:
  0.0 57.9 %shard_map.82 = f32[2,32,128]{2,1,0:T(8,128)S(1)} custom-call(s32[2,16]{1,0:T(2,128)} %bitcast.1, s32[2,16]{1,0:T(2,128)} %offs.1, f32[16]{0:T(128)} %defocus.1, s32[8]{0:T(128)} %counts.1, f32[8]{0:T(128)} %tilt.1, bf16[16,128,128]{2,1,0:T(8,128)(2,1)} %images_hbm.1, bf16[8,128,128]{2,1,0:T(8,128)(2,1)} %proj_hbm.1, bf16[384,128]{1,0:T(8,128)(2,1)} %constant.2.clone.table_hbm), custom_call_target="tpu_custom_call" | custom-call | tf_op jit(solution)/shard_map/pallas_call | solution.py:551
  57.9 0.6 %copy.10 = f32[2,32,128]{2,1,0:T(8,128)} copy(f32[2,32,128]{2,1,0:T(8,128)S(1)} %shard_map.82) | data formatting | bytes 65536

commit v7 on v6

--- a/solution.py
+++ b/solution.py
@@ -162,7 +162,8 @@
 
     def to_z(buf, send, recv, k):
         device = at_z(k)[1]
-        return pltpu.make_async_remote_copy(buf.at[z], buf.at[z], send.at[k], recv.at[k], device_id=device, device_id_type=MESH)
+        ref = buf.at[z, pl.ds(0, 2)]
+        return pltpu.make_async_remote_copy(ref, ref, send.at[k], recv.at[k], device_id=device, device_id_type=MESH)
 
     def ring(step, sign, send, recv):
         source = lax.rem(z + (nz - sign * (step // PIECES)), nz)

time: 58.6 us -> 58.5 us (level)
  no operation moved by 1% of the time
where the time goes in v7:
time: 58.5 us; the launch traced here: 58.4 us
  Pallas kernels  57.7 us (99%)
  local copies, waits for them, and re-layouts  0.62 us (1%)
    pallas_call x1, Pallas kernels, body(): pl.pallas_call(functools.partial(kernel, nz, nq, ns), out_shape=pltpu.VME...  57.7 us

profile of v7, /device:TPU:1, one launch (start us, length us, event | category | flops | bytes accessed | tf_op | source)
XLA Modules:
  0.0 58.4 jit_solution(6539537014181059036)
XLA Ops:
  0.0 57.7 %shard_map.82 = f32[2,32,128]{2,1,0:T(8,128)S(1)} custom-call(s32[2,16]{1,0:T(2,128)} %bitcast.1, s32[2,16]{1,0:T(2,128)} %offs.1, f32[16]{0:T(128)} %defocus.1, s32[8]{0:T(128)} %counts.1, f32[8]{0:T(128)} %tilt.1, bf16[16,128,128]{2,1,0:T(8,128)(2,1)} %images_hbm.1, bf16[8,128,128]{2,1,0:T(8,128)(2,1)} %proj_hbm.1, bf16[384,128]{1,0:T(8,128)(2,1)} %constant.2.clone.table_hbm), custom_call_target="tpu_custom_call" | custom-call | tf_op jit(solution)/shard_map/pallas_call | solution.py:552
  57.7 0.6 %copy.10 = f32[2,32,128]{2,1,0:T(8,128)} copy(f32[2,32,128]{2,1,0:T(8,128)S(1)} %shard_map.82) | data formatting | bytes 65536
